TPU v7x, 512 devices: a whole 4x4x16 slice. The times are simulated.
512 devices in a mesh: slab: 2 (over core), row: 16 (over z), col: 16 (over x, y).
Axes of the slice: x: 4, y: 4, z: 16, core: 2. Of those that a mesh axis runs over, the one named last changes fastest.
Arguments:
- video: bfloat16 [8, 128, 49152], P('slab', 'row', 'col'), may hold values from -40 to 40
- cache_in: bfloat16 [2, 128, 49152], P(None, 'row', 'col'), may hold values from -4 to 4
- cache_mid: bfloat16 [2, 128, 49152], P(None, 'row', 'col'), may hold values from -4 to 4
- gain_in: float32 [192], replicated, may hold values from 0.1 to 1.9
- gain_mid: float32 [192], replicated, may hold values from 0.1 to 1.9
- conv_in: bfloat16 [3, 3, 110592], replicated, may hold values from -0.078125 to 0.078125
- bias_in: float32 [192], replicated, may hold values from -3 to 3
- conv_mid: bfloat16 [3, 3, 110592], replicated, may hold values from -0.078125 to 0.078125
- bias_mid: float32 [192], replicated, may hold values from -3 to 3
Outputs:
- decoded: bfloat16 [8, 128, 49152], P('slab', 'row', 'col')
All inputs are finite; a program needn't handle non-finite values.
Results may differ from a plain program's by a relative error of at most 0.0022.
Values may be sent and summed in bfloat16 or wider, within the bound.
A program may use at most 64 MiB of HBM per device.

v0:
```python
import jax
import jax.numpy as jnp
from jax import lax
from jax.sharding import PartitionSpec as P


def with_halo(shard, sides, width):
    for axis, dim in sides:
        devices, length = (lax.axis_size(axis), shard.shape[dim])
        up = [(i, (i + 1) % devices) for i in range(devices - 1)]
        down = [(j, i) for i, j in up]
        last = lax.slice_in_dim(shard, length - width, length, axis=dim)
        initial = lax.slice_in_dim(shard, 0, width, axis=dim)
        before = lax.ppermute(last, axis, up)
        after = lax.ppermute(initial, axis, down)
        shard = jnp.concatenate([before, shard, after], axis=dim)
    return shard


def from_behind(value, axis, steps):
    count = lax.axis_size(axis)
    initial, last = (max(0, -steps), min(count, count - steps))
    return lax.ppermute(value, axis, [(source, source + steps) for source in range(initial, last)])


def activate(values, gain):
    values = values.astype(jnp.float32)
    mean_sq = jnp.mean(values * values, axis=-1, keepdims=True)
    return jax.nn.silu(values * lax.rsqrt(mean_sq + 1e-06) * gain)


def convolve(padded, kernel, bias):
    frames = padded.shape[0] - 2
    height = padded.shape[1] - 2
    width = padded.shape[2] - 2
    chans = padded.shape[3]
    outs = bias.shape[0]
    total = jnp.zeros((frames, height, width, outs), jnp.float32)
    for step_t in range(3):
        for step_h in range(3):
            rows = padded[step_t : step_t + frames, step_h : step_h + height]
            flat = rows.reshape(-1, chans)
            taps = kernel[step_t, step_h].reshape(3, chans, outs)
            taps = jnp.transpose(taps, (1, 0, 2)).reshape(chans, 3 * outs)
            product = jnp.dot(flat, taps, preferred_element_type=jnp.float32)
            product = product.reshape(frames, height, width + 2, 3 * outs)
            for q in range(3):
                total = total + product[:, :, q : q + width, q * outs : (q + 1) * outs]
    return total + bias


def tile_convolve(sequence, kernel, bias, exchange):
    padded = exchange(sequence)
    return convolve(padded, kernel, bias)


def rim_input(sequence):
    return with_halo(sequence, (("row", 1), ("col", 2)), 1)


def rim_middle(sequence):
    return with_halo(sequence, (("row", 1), ("col", 2)), 1)


def body(video, cache_in, cache_mid, gain_in, gain_mid, conv_in, bias_in, conv_mid, bias_mid):
    chans = gain_in.shape[0]
    slab_len = video.shape[0]
    tile_h = video.shape[1]
    tile_w = video.shape[2] // chans
    video = video.reshape(slab_len, tile_h, tile_w, chans)
    cache_in = cache_in.reshape(2, tile_h, tile_w, chans)
    cache_mid = cache_mid.reshape(2, tile_h, tile_w, chans)
    is_first = lax.axis_index("slab") == 0
    first = activate(video, gain_in).astype(jnp.bfloat16)
    earlier = from_behind(first[2:], "slab", 1)
    earlier = jnp.where(is_first, cache_in, earlier)
    seq_in = jnp.concatenate([earlier, first], axis=0)
    hidden = tile_convolve(seq_in, conv_in, bias_in, rim_input)
    middle = activate(hidden, gain_mid).astype(jnp.bfloat16)
    earlier_mid = from_behind(middle[2:], "slab", 1)
    earlier_mid = jnp.where(is_first, cache_mid, earlier_mid)
    seq_mid = jnp.concatenate([earlier_mid, middle], axis=0)
    branch = tile_convolve(seq_mid, conv_mid, bias_mid, rim_middle)
    result = (video.astype(jnp.float32) + branch).astype(jnp.bfloat16)
    return result.reshape(slab_len, tile_h, tile_w * chans)


def solution(mesh):
    in_specs = (
        P("slab", "row", "col"),
        P(None, "row", "col"),
        P(None, "row", "col"),
        P(),
        P(),
        P(),
        P(),
        P(),
        P(),
    )
    out_specs = P("slab", "row", "col")
    return jax.shard_map(body, mesh=mesh, in_specs=in_specs, out_specs=out_specs, check_vma=False)
```

profile of v0, /device:TPU:70, one launch (start us, length us, event | category | flops | bytes accessed | tf_op | source)
XLA Modules:
  0.0 158.1 jit_solution(8146263135189613764)
XLA Ops:
  3.1 2.4 %collective-permute-start = (bf16[2,8,16,192]{3,2,1,0:T(8,128)(2,1)}, bf16[2,8,16,192]{3,2,1,0:T(8,128)(2,1)}, u32[]{:S(2)}, u32[]{:S(2)}) collective-permute-start(bf16[2,8,16,192]{3,2,1,0:T(8,128)(2,1)} %slice.400), channel_id=1, source_target_pairs={{0,256},{1,257},{2,258},{3,259},{4,260},{5,261},{6,262},{7,263},{8... | collective-permute-start | bytes 294920 | tf_op jit(solution)/shard_map/ppermute | solution.py:23
  7.3 3.8 %collective-permute-start.1 = (bf16[6,1,16,192]{3,2,1,0:T(8,128)(2,1)S(1)}, bf16[6,1,16,192]{3,2,1,0:T(8,128)(2,1)S(1)}, u32[]{:S(2)}, u32[]{:S(2)}) collective-permute-start(bf16[6,1,16,192]{3,2,1,0:T(8,128)(2,1)S(1)} %get-tuple-element.31), channel_id=1, source_target_pairs={{0,16},{16,32},{32,48},{48,64},{64,80},{80,96},{96,112},{112,128},... | collective-permute-start | bytes 110600 | tf_op jit(solution)/shard_map/ppermute | solution.py:14
  11.2 2.0 %collective-permute-start.2 = (bf16[6,1,16,192]{3,2,1,0:T(8,128)(2,1)S(1)}, bf16[6,1,16,192]{3,2,1,0:T(8,128)(2,1)S(1)}, u32[]{:S(2)}, u32[]{:S(2)}) collective-permute-start(bf16[6,1,16,192]{3,2,1,0:T(8,128)(2,1)S(1)} %get-tuple-element.32), channel_id=1, source_target_pairs={{16,0},{32,16},{48,32},{64,48},{80,64},{96,80},{112,96},{128,112},... | collective-permute-start | bytes 110600 | tf_op jit(solution)/shard_map/ppermute | solution.py:15
  13.3 4.9 %collective-permute-done.2 = bf16[6,1,16,192]{3,2,1,0:T(8,128)(2,1)S(1)} collective-permute-done((bf16[6,1,16,192]{3,2,1,0:T(8,128)(2,1)S(1)}, bf16[6,1,16,192]{3,2,1,0:T(8,128)(2,1)S(1)}, u32[]{:S(2)}, u32[]{:S(2)}) %collective-permute-start.2) | collective-permute-done | bytes 36896 | tf_op jit(solution)/shard_map/ppermute | solution.py:15
  19.0 3.5 %collective-permute-start.3 = (bf16[6,10,1,192]{3,2,1,0:T(2,128)(2,1)}, bf16[6,10,1,192]{3,2,1,0:T(2,128)(2,1)}, u32[]{:S(2)}, u32[]{:S(2)}) collective-permute-start(bf16[6,10,1,192]{3,2,1,0:T(2,128)(2,1)} %get-tuple-element.27), channel_id=1, source_target_pairs={{0,1},{1,2},{2,3},{3,4},{4,5},{5,6},{6,7},{7,8},{8,9},{9,10},{10,1... | collective-permute-start | bytes 69128 | tf_op jit(solution)/shard_map/ppermute | solution.py:14
  22.5 4.5 %collective-permute-start.4 = (bf16[6,10,1,192]{3,2,1,0:T(2,128)(2,1)S(1)}, bf16[6,10,1,192]{3,2,1,0:T(2,128)(2,1)}, u32[]{:S(2)}, u32[]{:S(2)}) collective-permute-start(bf16[6,10,1,192]{3,2,1,0:T(2,128)(2,1)S(1)} %get-tuple-element.28), channel_id=1, source_target_pairs={{1,0},{2,1},{3,2},{4,3},{5,4},{6,5},{7,6},{8,7},{9,8},{10,9},{11,1... | collective-permute-start | bytes 69128 | tf_op jit(solution)/shard_map/ppermute | solution.py:15
  27.0 14.0 %slice_reduce_fusion.17 = (bf16[110592]{0:T(1024)(128)(2,1)}, bf16[110592]{0:T(1024)(128)(2,1)}, bf16[110592]{0:T(1024)(128)(2,1)}, bf16[110592]{0:T(1024)(128)(...) fusion(bf16[3,3,110592]{2,1,0:T(4,128)(2,1)S(1)} %copy-done), kind=kLoop, calls=%fused_computation.79 | loop fusion | bytes 3981312 | tf_op jit(solution)/shard_map/slice | solution.py:43
  53.1 1.6 fusion.21
  54.7 1.3 fusion.20
  57.4 2.6 %fusion.18 = f32[4,8,18,576]{3,2,1,0:T(8,128)} fusion(bf16[192,576,1,1]{0,1,3,2:T(8,128)(2,1)S(1)} %bitcast.116, bf16[6,10,1,192]{3,2,1,0:T(2,128)(2,1)} %collective-permute-done.4, bf16[6,1,16,192]{3,2,1,0:T(8,128)(2,1)S(1)} %copy-done.39, bf16[4,8,16,192]{3,2,1,0:T(8,128)(2,1)S(1)} %multiply_convert_fusion.1, bf16[2,8,16,192]{3,2,1,0:T(8,128)(2,1)S(1)} %copy-done.5, ...), kind=kOutput, calls=%fused_computation.110 | convolution fusion | flops 129890304 | bytes 1963008 | tf_op jit(solution)/shard_map/dot_general | solution.py:45
  60.0 2.6 %fusion.17 = f32[4,8,18,576]{3,2,1,0:T(8,128)} fusion(bf16[192,576,1,1]{0,1,3,2:T(8,128)(2,1)S(1)} %bitcast.118, bf16[6,10,1,192]{3,2,1,0:T(2,128)(2,1)} %collective-permute-done.4, bf16[6,1,16,192]{3,2,1,0:T(8,128)(2,1)S(1)} %copy-done.39, bf16[4,8,16,192]{3,2,1,0:T(8,128)(2,1)S(1)} %multiply_convert_fusion.1, bf16[2,8,16,192]{3,2,1,0:T(8,128)(2,1)S(1)} %copy-done.5, ...), kind=kOutput, calls=%fused_computation.109 | convolution fusion | flops 129890304 | bytes 1963008 | tf_op jit(solution)/shard_map/dot_general | solution.py:45
  62.6 2.6 %fusion.16 = f32[4,8,18,576]{3,2,1,0:T(8,128)} fusion(bf16[192,576,1,1]{0,1,3,2:T(8,128)(2,1)S(1)} %bitcast.120, bf16[6,10,1,192]{3,2,1,0:T(2,128)(2,1)} %collective-permute-done.4, bf16[6,1,16,192]{3,2,1,0:T(8,128)(2,1)S(1)} %copy-done.39, bf16[4,8,16,192]{3,2,1,0:T(8,128)(2,1)S(1)} %multiply_convert_fusion.1, bf16[2,8,16,192]{3,2,1,0:T(8,128)(2,1)S(1)} %copy-done.5, ...), kind=kOutput, calls=%fused_computation.108 | convolution fusion | flops 129890304 | bytes 1963008 | tf_op jit(solution)/shard_map/dot_general | solution.py:45
  65.3 2.6 %fusion.15 = f32[4,8,18,576]{3,2,1,0:T(8,128)} fusion(bf16[192,576,1,1]{0,1,3,2:T(8,128)(2,1)S(1)} %bitcast.124, bf16[6,10,1,192]{3,2,1,0:T(2,128)(2,1)} %collective-permute-done.4, bf16[6,1,16,192]{3,2,1,0:T(8,128)(2,1)S(1)} %copy-done.39, bf16[4,8,16,192]{3,2,1,0:T(8,128)(2,1)S(1)} %multiply_convert_fusion.1, bf16[2,8,16,192]{3,2,1,0:T(8,128)(2,1)S(1)} %copy-done.5, ...), kind=kOutput, calls=%fused_computation.107 | convolution fusion | flops 129890304 | bytes 1963008 | tf_op jit(solution)/shard_map/dot_general | solution.py:45
  67.9 2.7 %fusion.14 = f32[4,8,18,576]{3,2,1,0:T(8,128)} fusion(bf16[192,576,1,1]{0,1,3,2:T(8,128)(2,1)S(1)} %bitcast.126, bf16[6,10,1,192]{3,2,1,0:T(2,128)(2,1)} %collective-permute-done.4, bf16[6,1,16,192]{3,2,1,0:T(8,128)(2,1)S(1)} %copy-done.39, bf16[4,8,16,192]{3,2,1,0:T(8,128)(2,1)S(1)} %multiply_convert_fusion.1, bf16[2,8,16,192]{3,2,1,0:T(8,128)(2,1)S(1)} %copy-done.5, ...), kind=kOutput, calls=%fused_computation.106 | convolution fusion | flops 129890304 | bytes 1963008 | tf_op jit(solution)/shard_map/dot_general | solution.py:45
  70.6 2.6 %fusion.13 = f32[4,8,18,576]{3,2,1,0:T(8,128)} fusion(bf16[192,576,1,1]{0,1,3,2:T(8,128)(2,1)S(1)} %bitcast.122, bf16[6,10,1,192]{3,2,1,0:T(2,128)(2,1)} %collective-permute-done.4, bf16[6,1,16,192]{3,2,1,0:T(8,128)(2,1)S(1)} %copy-done.39, bf16[4,8,16,192]{3,2,1,0:T(8,128)(2,1)S(1)} %multiply_convert_fusion.1, bf16[2,8,16,192]{3,2,1,0:T(8,128)(2,1)S(1)} %copy-done.5, ...), kind=kOutput, calls=%fused_computation.105 | convolution fusion | flops 129890304 | bytes 1963008 | tf_op jit(solution)/shard_map/dot_general | solution.py:45
  73.2 7.6 %multiply_reduce_fusion = (f32[4,8,16]{2,1,0:T(8,128)S(1)}, f32[4,8,16,192]{3,2,1,0:T(8,128)S(1)}) fusion(f32[192]{0:T(256)S(1)} %copy-done.42, f32[4,8,18,576]{3,2,1,0:T(8,128)} %fusion.13, f32[4,8,18,576]{3,2,1,0:T(8,128)} %fusion.14, f32[4,8,18,576]{3,2,1,0:T(8,128)} %fusion.15, f32[4,8,18,576]{3,2,1,0:T(8,128)} %fusion.16, f32[4,8,18,576]{3,2,1,0:T(8,128)} %fusion.17, ...), kind=kLoop, calls=%fused_computation.59 | loop fusion | flops 2850304 | bytes 11012864 | tf_op jit(solution)/shard_map/reduce_sum | solution.py:28
  81.7 1.9 %collective-permute-start.5 = (bf16[2,8,16,192]{3,2,1,0:T(8,128)(2,1)}, bf16[2,8,16,192]{3,2,1,0:T(8,128)(2,1)}, u32[]{:S(2)}, u32[]{:S(2)}) collective-permute-start(bf16[2,8,16,192]{3,2,1,0:T(8,128)(2,1)} %slice.428), channel_id=1, source_target_pairs={{0,256},{1,257},{2,258},{3,259},{4,260},{5,261},{6,262},{7,263},{8... | collective-permute-start | bytes 294920 | tf_op jit(solution)/shard_map/ppermute | solution.py:23
  85.5 5.1 %collective-permute-start.6 = (bf16[6,1,16,192]{3,2,1,0:T(8,128)(2,1)S(1)}, bf16[6,1,16,192]{3,2,1,0:T(8,128)(2,1)S(1)}, u32[]{:S(2)}, u32[]{:S(2)}) collective-permute-start(bf16[6,1,16,192]{3,2,1,0:T(8,128)(2,1)S(1)} %get-tuple-element.29), channel_id=1, source_target_pairs={{0,16},{16,32},{32,48},{48,64},{64,80},{80,96},{96,112},{112,128},... | collective-permute-start | bytes 110600 | tf_op jit(solution)/shard_map/ppermute | solution.py:14
  90.6 1.9 %collective-permute-start.7 = (bf16[6,1,16,192]{3,2,1,0:T(8,128)(2,1)S(1)}, bf16[6,1,16,192]{3,2,1,0:T(8,128)(2,1)S(1)}, u32[]{:S(2)}, u32[]{:S(2)}) collective-permute-start(bf16[6,1,16,192]{3,2,1,0:T(8,128)(2,1)S(1)} %get-tuple-element.30), channel_id=1, source_target_pairs={{16,0},{32,16},{48,32},{64,48},{80,64},{96,80},{112,96},{128,112},... | collective-permute-start | bytes 110600 | tf_op jit(solution)/shard_map/ppermute | solution.py:15
  92.6 4.0 %collective-permute-done.7 = bf16[6,1,16,192]{3,2,1,0:T(8,128)(2,1)S(1)} collective-permute-done((bf16[6,1,16,192]{3,2,1,0:T(8,128)(2,1)S(1)}, bf16[6,1,16,192]{3,2,1,0:T(8,128)(2,1)S(1)}, u32[]{:S(2)}, u32[]{:S(2)}) %collective-permute-start.7) | collective-permute-done | bytes 36896 | tf_op jit(solution)/shard_map/ppermute | solution.py:15
  97.3 1.9 %collective-permute-start.8 = (bf16[6,10,1,192]{3,2,1,0:T(2,128)(2,1)}, bf16[6,10,1,192]{3,2,1,0:T(2,128)(2,1)}, u32[]{:S(2)}, u32[]{:S(2)}) collective-permute-start(bf16[6,10,1,192]{3,2,1,0:T(2,128)(2,1)} %get-tuple-element.25), channel_id=1, source_target_pairs={{0,1},{1,2},{2,3},{3,4},{4,5},{5,6},{6,7},{7,8},{8,9},{9,10},{10,1... | collective-permute-start | bytes 69128 | tf_op jit(solution)/shard_map/ppermute | solution.py:14
  99.3 6.0 %collective-permute-start.9 = (bf16[6,10,1,192]{3,2,1,0:T(2,128)(2,1)S(1)}, bf16[6,10,1,192]{3,2,1,0:T(2,128)(2,1)}, u32[]{:S(2)}, u32[]{:S(2)}) collective-permute-start(bf16[6,10,1,192]{3,2,1,0:T(2,128)(2,1)S(1)} %get-tuple-element.26), channel_id=1, source_target_pairs={{1,0},{2,1},{3,2},{4,3},{5,4},{6,5},{7,6},{8,7},{9,8},{10,9},{11,1... | collective-permute-start | bytes 69128 | tf_op jit(solution)/shard_map/ppermute | solution.py:15
  105.3 14.1 %slice_reduce_fusion.8 = (bf16[110592]{0:T(1024)(128)(2,1)}, bf16[110592]{0:T(1024)(128)(2,1)}, bf16[110592]{0:T(1024)(128)(2,1)}, bf16[110592]{0:T(1024)(128)(2...) fusion(bf16[3,3,110592]{2,1,0:T(4,128)(2,1)S(1)} %copy-done.1), kind=kLoop, calls=%fused_computation.70 | loop fusion | bytes 3981312 | tf_op jit(solution)/shard_map/slice | solution.py:43
  131.4 1.6 fusion.12
  133.0 1.3 fusion.11
  135.7 1.3 fusion.9
  137.1 2.6 %fusion.8 = f32[4,8,18,576]{3,2,1,0:T(8,128)} fusion(bf16[192,576,1,1]{0,1,3,2:T(8,128)(2,1)S(1)} %bitcast.119, bf16[6,10,1,192]{3,2,1,0:T(2,128)(2,1)} %collective-permute-done.9, bf16[6,1,16,192]{3,2,1,0:T(8,128)(2,1)S(1)} %copy-done.41, bf16[4,8,16,192]{3,2,1,0:T(8,128)(2,1)S(1)} %multiply_convert_fusion, bf16[2,8,16,192]{3,2,1,0:T(8,128)(2,1)S(1)} %copy-done.3, ...), kind=kOutput, calls=%fused_computation.100 | convolution fusion | flops 129890304 | bytes 1963008 | tf_op jit(solution)/shard_map/dot_general | solution.py:45
  139.7 2.6 %fusion.7 = f32[4,8,18,576]{3,2,1,0:T(8,128)} fusion(bf16[192,576,1,1]{0,1,3,2:T(8,128)(2,1)S(1)} %bitcast.121, bf16[6,10,1,192]{3,2,1,0:T(2,128)(2,1)} %collective-permute-done.9, bf16[6,1,16,192]{3,2,1,0:T(8,128)(2,1)S(1)} %copy-done.41, bf16[4,8,16,192]{3,2,1,0:T(8,128)(2,1)S(1)} %multiply_convert_fusion, bf16[2,8,16,192]{3,2,1,0:T(8,128)(2,1)S(1)} %copy-done.3, ...), kind=kOutput, calls=%fused_computation.99 | convolution fusion | flops 129890304 | bytes 1963008 | tf_op jit(solution)/shard_map/dot_general | solution.py:45
  142.3 2.6 %fusion.6 = f32[4,8,18,576]{3,2,1,0:T(8,128)} fusion(bf16[192,576,1,1]{0,1,3,2:T(8,128)(2,1)S(1)} %bitcast.125, bf16[6,10,1,192]{3,2,1,0:T(2,128)(2,1)} %collective-permute-done.9, bf16[6,1,16,192]{3,2,1,0:T(8,128)(2,1)S(1)} %copy-done.41, bf16[4,8,16,192]{3,2,1,0:T(8,128)(2,1)S(1)} %multiply_convert_fusion, bf16[2,8,16,192]{3,2,1,0:T(8,128)(2,1)S(1)} %copy-done.3, ...), kind=kOutput, calls=%fused_computation.98 | convolution fusion | flops 129890304 | bytes 1963008 | tf_op jit(solution)/shard_map/dot_general | solution.py:45
  145.0 2.6 %fusion.5 = f32[4,8,18,576]{3,2,1,0:T(8,128)} fusion(bf16[192,576,1,1]{0,1,3,2:T(8,128)(2,1)S(1)} %bitcast.127, bf16[6,10,1,192]{3,2,1,0:T(2,128)(2,1)} %collective-permute-done.9, bf16[6,1,16,192]{3,2,1,0:T(8,128)(2,1)S(1)} %copy-done.41, bf16[4,8,16,192]{3,2,1,0:T(8,128)(2,1)S(1)} %multiply_convert_fusion, bf16[2,8,16,192]{3,2,1,0:T(8,128)(2,1)S(1)} %copy-done.3, ...), kind=kOutput, calls=%fused_computation.97 | convolution fusion | flops 129890304 | bytes 1963008 | tf_op jit(solution)/shard_map/dot_general | solution.py:45
  147.6 2.7 %fusion.4 = f32[4,8,18,576]{3,2,1,0:T(8,128)} fusion(bf16[192,576,1,1]{0,1,3,2:T(8,128)(2,1)S(1)} %bitcast.123, bf16[6,10,1,192]{3,2,1,0:T(2,128)(2,1)} %collective-permute-done.9, bf16[6,1,16,192]{3,2,1,0:T(8,128)(2,1)S(1)} %copy-done.41, bf16[4,8,16,192]{3,2,1,0:T(8,128)(2,1)S(1)} %multiply_convert_fusion, bf16[2,8,16,192]{3,2,1,0:T(8,128)(2,1)S(1)} %copy-done.3, ...), kind=kOutput, calls=%fused_computation.96 | convolution fusion | flops 129890304 | bytes 1963008 | tf_op jit(solution)/shard_map/dot_general | solution.py:45
  150.3 6.8 %fusion.2 = bf16[4,8,16,192]{3,2,1,0:T(8,128)(2,1)S(1)} fusion(f32[4,8,16,192]{3,2,1,0:T(8,128)S(1)} %reshape.179, f32[4,8,18,576]{3,2,1,0:T(8,128)} %fusion.4, f32[4,8,18,576]{3,2,1,0:T(8,128)} %fusion.5, f32[4,8,18,576]{3,2,1,0:T(8,128)} %fusion.6, f32[4,8,18,576]{3,2,1,0:T(8,128)} %fusion.7, f32[4,8,18,576]{3,2,1,0:T(8,128)} %fusion.8, ...), kind=kLoop, calls=%fused_computation.5 | loop fusion | flops 2850816 | bytes 11207424 | tf_op jit(solution)/shard_map/convert_element_type | solution.py:84
  (153 shorter events, 36.6 us)
Async XLA Ops:
  0.0 5.5 %copy-start.36 = (bf16[2,8,3072]{2,1,0:T(8,128)(2,1)S(1)}, bf16[2,8,3072]{2,1,0:T(8,128)(2,1)}, u32[]{:S(2)}) copy-start(bf16[2,8,3072]{2,1,0:T(8,128)(2,1)} %param.10) | copy-start | bytes 294916
  1.4 25.6 %copy-start = (bf16[3,3,110592]{2,1,0:T(4,128)(2,1)S(1)}, bf16[3,3,110592]{2,1,0:T(4,128)(2,1)}, u32[]{:S(2)}) copy-start(bf16[3,3,110592]{2,1,0:T(4,128)(2,1)} %param.14) | copy-start | bytes 5971972
  3.1 3.2 %collective-permute-start = (bf16[2,8,16,192]{3,2,1,0:T(8,128)(2,1)}, bf16[2,8,16,192]{3,2,1,0:T(8,128)(2,1)}, u32[]{:S(2)}, u32[]{:S(2)}) collective-permute-start(bf16[2,8,16,192]{3,2,1,0:T(8,128)(2,1)} %slice.400), channel_id=1, source_target_pairs={{0,256},{1,257},{2,258},{3,259},{4,260},{5,261},{6,262},{7,263},{8... | collective-permute-start | bytes 294920 | tf_op jit(solution)/shard_map/ppermute | solution.py:23
  7.3 11.0 %copy-start.4 = (bf16[2,8,16,192]{3,2,1,0:T(8,128)(2,1)}, bf16[2,8,16,192]{3,2,1,0:T(8,128)(2,1)S(1)}, u32[]{:S(2)}) copy-start(bf16[2,8,16,192]{3,2,1,0:T(8,128)(2,1)S(1)} %broadcast_select_fusion.1) | copy-start | bytes 294916
  7.3 6.0 %collective-permute-start.1 = (bf16[6,1,16,192]{3,2,1,0:T(8,128)(2,1)S(1)}, bf16[6,1,16,192]{3,2,1,0:T(8,128)(2,1)S(1)}, u32[]{:S(2)}, u32[]{:S(2)}) collective-permute-start(bf16[6,1,16,192]{3,2,1,0:T(8,128)(2,1)S(1)} %get-tuple-element.31), channel_id=1, source_target_pairs={{0,16},{16,32},{32,48},{48,64},{64,80},{80,96},{96,112},{112,128},... | collective-permute-start | bytes 110600 | tf_op jit(solution)/shard_map/ppermute | solution.py:14
  11.2 7.1 %collective-permute-start.2 = (bf16[6,1,16,192]{3,2,1,0:T(8,128)(2,1)S(1)}, bf16[6,1,16,192]{3,2,1,0:T(8,128)(2,1)S(1)}, u32[]{:S(2)}, u32[]{:S(2)}) collective-permute-start(bf16[6,1,16,192]{3,2,1,0:T(8,128)(2,1)S(1)} %get-tuple-element.32), channel_id=1, source_target_pairs={{16,0},{32,16},{48,32},{64,48},{80,64},{96,80},{112,96},{128,112},... | collective-permute-start | bytes 110600 | tf_op jit(solution)/shard_map/ppermute | solution.py:15
  18.3 4.2 %copy-start.38 = (bf16[6,1,16,192]{3,2,1,0:T(8,128)(2,1)}, bf16[6,1,16,192]{3,2,1,0:T(8,128)(2,1)S(1)}, u32[]{:S(2)}) copy-start(bf16[6,1,16,192]{3,2,1,0:T(8,128)(2,1)S(1)} %collective-permute-done.2) | copy-start | bytes 110596
  19.0 34.0 %collective-permute-start.3 = (bf16[6,10,1,192]{3,2,1,0:T(2,128)(2,1)}, bf16[6,10,1,192]{3,2,1,0:T(2,128)(2,1)}, u32[]{:S(2)}, u32[]{:S(2)}) collective-permute-start(bf16[6,10,1,192]{3,2,1,0:T(2,128)(2,1)} %get-tuple-element.27), channel_id=1, source_target_pairs={{0,1},{1,2},{2,3},{3,4},{4,5},{5,6},{6,7},{7,8},{8,9},{9,10},{10,1... | collective-permute-start | bytes 69128 | tf_op jit(solution)/shard_map/ppermute | solution.py:14
  22.5 30.5 %collective-permute-start.4 = (bf16[6,10,1,192]{3,2,1,0:T(2,128)(2,1)S(1)}, bf16[6,10,1,192]{3,2,1,0:T(2,128)(2,1)}, u32[]{:S(2)}, u32[]{:S(2)}) collective-permute-start(bf16[6,10,1,192]{3,2,1,0:T(2,128)(2,1)S(1)} %get-tuple-element.28), channel_id=1, source_target_pairs={{1,0},{2,1},{3,2},{4,3},{5,4},{6,5},{7,6},{8,7},{9,8},{10,9},{11,1... | collective-permute-start | bytes 69128 | tf_op jit(solution)/shard_map/ppermute | solution.py:15
  41.0 4.1 %copy-start.18 = (bf16[110592]{0:T(1024)(128)(2,1)S(1)}, bf16[110592]{0:T(1024)(128)(2,1)}, u32[]{:S(2)}) copy-start(bf16[110592]{0:T(1024)(128)(2,1)} %get-tuple-element.19) | copy-start | bytes 663556
  42.2 4.1 %copy-start.16 = (bf16[110592]{0:T(1024)(128)(2,1)S(1)}, bf16[110592]{0:T(1024)(128)(2,1)}, u32[]{:S(2)}) copy-start(bf16[110592]{0:T(1024)(128)(2,1)} %get-tuple-element.18) | copy-start | bytes 663556
  45.4 3.1 %copy-start.12 = (bf16[110592]{0:T(1024)(128)(2,1)S(1)}, bf16[110592]{0:T(1024)(128)(2,1)}, u32[]{:S(2)}) copy-start(bf16[110592]{0:T(1024)(128)(2,1)} %get-tuple-element.16) | copy-start | bytes 663556
  46.5 3.2 %copy-start.10 = (bf16[110592]{0:T(1024)(128)(2,1)S(1)}, bf16[110592]{0:T(1024)(128)(2,1)}, u32[]{:S(2)}) copy-start(bf16[110592]{0:T(1024)(128)(2,1)} %get-tuple-element.15) | copy-start | bytes 663556
  47.6 3.2 %copy-start.8 = (bf16[110592]{0:T(1024)(128)(2,1)S(1)}, bf16[110592]{0:T(1024)(128)(2,1)}, u32[]{:S(2)}) copy-start(bf16[110592]{0:T(1024)(128)(2,1)} %get-tuple-element.22) | copy-start | bytes 663556
  48.7 3.2 %copy-start.6 = (bf16[110592]{0:T(1024)(128)(2,1)S(1)}, bf16[110592]{0:T(1024)(128)(2,1)}, u32[]{:S(2)}) copy-start(bf16[110592]{0:T(1024)(128)(2,1)} %get-tuple-element.21) | copy-start | bytes 663556
  49.8 3.2 %copy-start.5 = (bf16[2,8,16,192]{3,2,1,0:T(8,128)(2,1)S(1)}, bf16[2,8,16,192]{3,2,1,0:T(8,128)(2,1)}, u32[]{:S(2)}) copy-start(bf16[2,8,16,192]{3,2,1,0:T(8,128)(2,1)} %copy-done.4) | copy-start | bytes 294916
  49.9 3.2 %copy-start.39 = (bf16[6,1,16,192]{3,2,1,0:T(8,128)(2,1)S(1)}, bf16[6,1,16,192]{3,2,1,0:T(8,128)(2,1)}, u32[]{:S(2)}) copy-start(bf16[6,1,16,192]{3,2,1,0:T(8,128)(2,1)} %copy-done.38) | copy-start | bytes 110596
  73.2 7.6 %copy-start.43 = (f32[192]{0:T(256)S(1)}, f32[192]{0:T(256)}, u32[]{:S(2)}) copy-start(f32[192]{0:T(256)} %param.13) | copy-start | bytes 2308
  73.2 10.4 %copy-start.37 = (bf16[2,8,3072]{2,1,0:T(8,128)(2,1)S(1)}, bf16[2,8,3072]{2,1,0:T(8,128)(2,1)}, u32[]{:S(2)}) copy-start(bf16[2,8,3072]{2,1,0:T(8,128)(2,1)} %param.11) | copy-start | bytes 294916
  80.8 24.5 %copy-start.1 = (bf16[3,3,110592]{2,1,0:T(4,128)(2,1)S(1)}, bf16[3,3,110592]{2,1,0:T(4,128)(2,1)}, u32[]{:S(2)}) copy-start(bf16[3,3,110592]{2,1,0:T(4,128)(2,1)} %param.16) | copy-start | bytes 5971972
  81.7 2.8 %collective-permute-start.5 = (bf16[2,8,16,192]{3,2,1,0:T(8,128)(2,1)}, bf16[2,8,16,192]{3,2,1,0:T(8,128)(2,1)}, u32[]{:S(2)}, u32[]{:S(2)}) collective-permute-start(bf16[2,8,16,192]{3,2,1,0:T(8,128)(2,1)} %slice.428), channel_id=1, source_target_pairs={{0,256},{1,257},{2,258},{3,259},{4,260},{5,261},{6,262},{7,263},{8... | collective-permute-start | bytes 294920 | tf_op jit(solution)/shard_map/ppermute | solution.py:23
  85.4 11.2 %copy-start.2 = (bf16[2,8,16,192]{3,2,1,0:T(8,128)(2,1)}, bf16[2,8,16,192]{3,2,1,0:T(8,128)(2,1)S(1)}, u32[]{:S(2)}) copy-start(bf16[2,8,16,192]{3,2,1,0:T(8,128)(2,1)S(1)} %broadcast_select_fusion) | copy-start | bytes 294916
  85.5 7.1 %collective-permute-start.6 = (bf16[6,1,16,192]{3,2,1,0:T(8,128)(2,1)S(1)}, bf16[6,1,16,192]{3,2,1,0:T(8,128)(2,1)S(1)}, u32[]{:S(2)}, u32[]{:S(2)}) collective-permute-start(bf16[6,1,16,192]{3,2,1,0:T(8,128)(2,1)S(1)} %get-tuple-element.29), channel_id=1, source_target_pairs={{0,16},{16,32},{32,48},{48,64},{64,80},{80,96},{96,112},{112,128},... | collective-permute-start | bytes 110600 | tf_op jit(solution)/shard_map/ppermute | solution.py:14
  90.6 6.0 %collective-permute-start.7 = (bf16[6,1,16,192]{3,2,1,0:T(8,128)(2,1)S(1)}, bf16[6,1,16,192]{3,2,1,0:T(8,128)(2,1)S(1)}, u32[]{:S(2)}, u32[]{:S(2)}) collective-permute-start(bf16[6,1,16,192]{3,2,1,0:T(8,128)(2,1)S(1)} %get-tuple-element.30), channel_id=1, source_target_pairs={{16,0},{32,16},{48,32},{64,48},{80,64},{96,80},{112,96},{128,112},... | collective-permute-start | bytes 110600 | tf_op jit(solution)/shard_map/ppermute | solution.py:15
  97.3 34.0 %collective-permute-start.8 = (bf16[6,10,1,192]{3,2,1,0:T(2,128)(2,1)}, bf16[6,10,1,192]{3,2,1,0:T(2,128)(2,1)}, u32[]{:S(2)}, u32[]{:S(2)}) collective-permute-start(bf16[6,10,1,192]{3,2,1,0:T(2,128)(2,1)} %get-tuple-element.25), channel_id=1, source_target_pairs={{0,1},{1,2},{2,3},{3,4},{4,5},{5,6},{6,7},{7,8},{8,9},{9,10},{10,1... | collective-permute-start | bytes 69128 | tf_op jit(solution)/shard_map/ppermute | solution.py:14
  99.3 32.1 %collective-permute-start.9 = (bf16[6,10,1,192]{3,2,1,0:T(2,128)(2,1)S(1)}, bf16[6,10,1,192]{3,2,1,0:T(2,128)(2,1)}, u32[]{:S(2)}, u32[]{:S(2)}) collective-permute-start(bf16[6,10,1,192]{3,2,1,0:T(2,128)(2,1)S(1)} %get-tuple-element.26), channel_id=1, source_target_pairs={{1,0},{2,1},{3,2},{4,3},{5,4},{6,5},{7,6},{8,7},{9,8},{10,9},{11,1... | collective-permute-start | bytes 69128 | tf_op jit(solution)/shard_map/ppermute | solution.py:15
  119.4 4.1 %copy-start.19 = (bf16[110592]{0:T(1024)(128)(2,1)S(1)}, bf16[110592]{0:T(1024)(128)(2,1)}, u32[]{:S(2)}) copy-start(bf16[110592]{0:T(1024)(128)(2,1)} %get-tuple-element.10) | copy-start | bytes 663556
  120.6 4.1 %copy-start.17 = (bf16[110592]{0:T(1024)(128)(2,1)S(1)}, bf16[110592]{0:T(1024)(128)(2,1)}, u32[]{:S(2)}) copy-start(bf16[110592]{0:T(1024)(128)(2,1)} %get-tuple-element.9) | copy-start | bytes 663556
  126.0 3.2 %copy-start.9 = (bf16[110592]{0:T(1024)(128)(2,1)S(1)}, bf16[110592]{0:T(1024)(128)(2,1)}, u32[]{:S(2)}) copy-start(bf16[110592]{0:T(1024)(128)(2,1)} %get-tuple-element.13) | copy-start | bytes 663556
  127.1 3.1 %copy-start.7 = (bf16[110592]{0:T(1024)(128)(2,1)S(1)}, bf16[110592]{0:T(1024)(128)(2,1)}, u32[]{:S(2)}) copy-start(bf16[110592]{0:T(1024)(128)(2,1)} %get-tuple-element.12) | copy-start | bytes 663556
  128.2 3.2 %copy-start.3 = (bf16[2,8,16,192]{3,2,1,0:T(8,128)(2,1)S(1)}, bf16[2,8,16,192]{3,2,1,0:T(8,128)(2,1)}, u32[]{:S(2)}) copy-start(bf16[2,8,16,192]{3,2,1,0:T(8,128)(2,1)} %copy-done.2) | copy-start | bytes 294916
  128.2 3.1 %copy-start.41 = (bf16[6,1,16,192]{3,2,1,0:T(8,128)(2,1)S(1)}, bf16[6,1,16,192]{3,2,1,0:T(8,128)(2,1)}, u32[]{:S(2)}) copy-start(bf16[6,1,16,192]{3,2,1,0:T(8,128)(2,1)} %copy-done.40) | copy-start | bytes 110596
  (23 other events, 54.2 us)
where the time goes:
time: 159 us; the launch traced here: 158 us
  local copies, waits for them, and re-layouts  57.1 us (36%)
  matrix products  38.8 us (24%)
  starting transfers between devices  33.1 us (21%)
  other arithmetic  19.2 us (12%)
  waiting for transfers between devices  9.14 us (6%)
    dot_general x18, matrix products, convolve(): product = jnp.dot(flat, taps, preferred_element_type=jnp.float32)  38.8 us
    slice x2, local copies, waits for them, and re-layouts, convolve(): taps = kernel[step_t, step_h].reshape(3, chans, outs)  28.1 us
    another operation x36, local copies, waits for them, and re-layouts, convolve(): taps = kernel[step_t, step_h].reshape(3, chans, outs)  23.6 us
    ppermute x4, starting transfers between devices, with_halo(): after = lax.ppermute(initial, axis, down)  14.4 us
    ppermute x4, starting transfers between devices, with_halo(): before = lax.ppermute(last, axis, up)  14.3 us
    ppermute x4, waiting for transfers between devices, with_halo(): after = lax.ppermute(initial, axis, down)  9 us
    reduce_sum x2, other arithmetic, activate(): mean_sq = jnp.mean(values * values, axis=-1, keepdims=True)  7.7 us
    convert_element_type x1, other arithmetic, body(): result = (video.astype(jnp.float32) + branch).astype(jnp.bfloat16)  6.85 us
  transfers between devices with their start and end apart: 10, of which 3 were waited for; matrix products, arithmetic and copies ran while one was open for 34% of the time, Pallas kernels for 0%

commit v1 on v0

v1 whole, which is shorter than its diff:
```python
import functools

import jax
import jax.numpy as jnp
from jax import lax
from jax.experimental import pallas as pl
from jax.experimental.pallas import tpu as pltpu
from jax.sharding import PartitionSpec as P

F32 = jnp.float32
BF16 = jnp.bfloat16
CHAN = 192
PITCH = 20
ROWS_IN, COLS_IN = 12, 20
ROWS_MID, COLS_MID = 10, 18
EARLY_IN = 30
EARLY_MID = 26
AROUND = [(-1, 0), (1, 0), (0, -1), (0, 1), (-1, -1), (-1, 1), (1, -1), (1, 1)]


def low_lanes(shape):
    return lax.broadcasted_iota(jnp.int32, shape, len(shape) - 1) < 64


def low_subs(shape):
    return lax.broadcasted_iota(jnp.int32, shape, len(shape) - 2) < 4


def swap(x):
    return pltpu.roll(x, 64, 1)


def act(a, b, gain_a, gain_b, lanes):
    square = a * a + jnp.where(lanes, b * b, 0.0)
    mean = jnp.sum(square, axis=1, keepdims=True) * (1.0 / CHAN)
    scale = lax.rsqrt(mean + 1e-6)
    ua, ub = a * scale * gain_a, b * scale * gain_b
    return ua / (1.0 + jnp.exp(-ua)), ub / (1.0 + jnp.exp(-ub))


def order_channels(order):
    c = lax.broadcasted_iota(jnp.int32, (256, 256), 0)
    o = lax.broadcasted_iota(jnp.int32, (256, 256), 1)
    o = jnp.where(o < CHAN, o, o - 64)
    r = o & 15
    source = (o - r) + jnp.where(r < 8, 2 * r, 2 * r - 15)
    order[...] = jnp.where(c == source, 1.0, 0.0).astype(BF16)


def lay_out_weights(raw, wide, out):
    per = wide.shape[0] // 24
    lanes = low_lanes((8, 128))
    flat = wide.reshape(wide.shape[0] * 8, 128)
    out[:, 13 * 128 : 13 * 128 + 64, :] = jnp.zeros((3, 64, 256), BF16)

    def step(n, _):
        a, part = n // (36 // per), n % (36 // per)
        for u in range(per):
            g = part * per + u
            wide[pl.ds(u * 24, 24), 0:3, :] = raw[a, pl.ds(g * 24, 24)].astype(F32)
            q, group = g // 12, g % 12
            for p in range(3):
                first = flat[pl.ds(u * 192 + p, 8, stride=24)]
                both = flat[pl.ds(u * 192 + 8 + p, 8, stride=24)]
                second = swap(flat[pl.ds(u * 192 + 16 + p, 8, stride=24)])
                odd = jnp.where(lanes, swap(both), second)
                row_a = (p * 3 + q) * 128 + 16 * group
                row_b = (9 + q) * 128 + 64 * p if p < 2 else 12 * 128 + 64 * q + jnp.where(q == 2, 64, 0)
                row = jnp.where(group < 8, row_a, row_b + 16 * (group - 8))
                row = pl.multiple_of(row, 16)
                out[a, pl.ds(row, 16), 0:128] = jnp.concatenate([first, odd], 0).astype(BF16)
                out[a, pl.ds(row, 16), 128:256] = jnp.concatenate([both, second], 0).astype(BF16)
        return 0

    lax.fori_loop(0, 3 * 36 // per, step, 0)


def pack_early(sa, sb, early, groups):
    lanes = low_lanes((16, 128))

    def frames(s, g):
        start = pl.multiple_of(g * 64, 64)
        return jnp.concatenate([s[pl.ds(start + 4, 8, stride=8)], s[pl.ds(start + 5, 8, stride=8)]], 0)

    def step(g, _):
        early[g] = frames(sa, g).astype(BF16)
        early[g + groups // 2] = frames(sa, g + groups // 2).astype(BF16)
        early[g + groups] = jnp.where(lanes, frames(sb, g), frames(sb, g + groups // 2)).astype(BF16)
        return 0

    lax.fori_loop(0, groups // 2, step, 0)


def unpack_early(sa, sb, early, groups):
    lanes = low_lanes((16, 128))

    def put(s, g, x):
        start = pl.multiple_of(g * 64, 64)
        s[pl.ds(start, 8, stride=8)] = x[0:8]
        s[pl.ds(start + 1, 8, stride=8)] = x[8:16]

    def step(g, _):
        put(sa, g, early[g].astype(F32))
        put(sa, g + groups // 2, early[g + groups // 2].astype(F32))
        b = early[g + groups].astype(F32)
        other = swap(b)
        put(sb, g, jnp.where(lanes, b, other))
        put(sb, g + groups // 2, jnp.where(lanes, other, b))
        return 0

    lax.fori_loop(0, groups // 2, step, 0)


def gather_taps(sa, sb, ta, tb, zp, zq, a, up, left, rows, cols):
    subs = low_subs((8, 128))
    lanes = low_lanes((16, 128))

    def pair(s, start, i, j):
        first = s[pl.ds(start + (i * PITCH + j) * 8 + a, 8), :]
        second = s[pl.ds(start + (i * PITCH + j + left) * 8 + a - 4, 8), :]
        return jnp.where(subs, first, second)

    def quad(s, start, j):
        return jnp.concatenate([pair(s, start, 0, j), pair(s, start, up, j)], 0).astype(BF16)

    def step(i, _):
        start = pl.multiple_of(i * (PITCH * 8), 8)
        for j in range(cols):
            ta[a, i, j] = quad(sa, start, j)
            tb[a, i, j] = quad(sb, start, j)
        return 0

    lax.fori_loop(0, rows, step, 0)

    def merge(i, _):
        for j in range(cols):
            zp[a, i, j] = jnp.where(lanes, tb[a, i, j], tb[a, i + 1, j])
        for j in range(cols - 1):
            zq[a, i, j] = jnp.where(lanes, tb[a, i + 2, j], tb[a, i + 2, j + 1])
        return 0

    lax.fori_loop(0, rows - 2, merge, 0)


def tap_columns(ta, zp, zq, a, rows, cols):
    parts = [ta[a, p : p + rows, q : q + cols] for p in range(3) for q in range(3)]
    parts += [zp[a, 0:rows, q : q + cols] for q in range(3)]
    parts += [zq[a, 0:rows, q : q + cols] for q in range(2)]
    return [x.reshape(rows * cols * 16, 128) for x in parts]


def convolve(ta, zp, zq, weights, times, rows, cols):
    columns = sum([tap_columns(ta, zp, zq, a, rows, cols) for a in times], [])
    weight = weights[times[0] : times[-1] + 1].reshape(len(times) * 14 * 128, 256)
    return jnp.dot(jnp.concatenate(columns, 1), weight, preferred_element_type=F32)


def kernel(sizes, video_hbm, cin_hbm, cmid_hbm, gain_in, gain_mid, win_hbm, bias_in, wmid_hbm, bias_mid, out,
           video, cin, cmid, raw_in, raw_mid, w_in, w_mid, wide, natural, mixed, order, sa, sb, s2a, s2b,
           units, early_in, early_mid, ta, tb, zp, zq, total,
           load_sem, send_sem, recv_sem, early_send, early_recv):
    n_row, n_col = sizes
    slab, row, col = lax.axis_index("slab"), lax.axis_index("row"), lax.axis_index("col")
    loads = [pltpu.make_async_copy(src, dst, load_sem.at[n]) for n, (src, dst) in enumerate(
        [(video_hbm, video), (cin_hbm, cin), (cmid_hbm, cmid), (win_hbm, raw_in), (wmid_hbm, raw_mid)])]
    for load in loads:
        load.start()

    def neighbour(dr, dc):
        return (slab, lax.rem(row + dr + n_row, n_row), lax.rem(col + dc + n_col, n_col))

    barrier = pltpu.get_barrier_semaphore()
    for dr, dc in AROUND:
        pl.semaphore_signal(barrier, inc=1, device_id=neighbour(dr, dc), device_id_type=pl.DeviceIdType.MESH)
    pl.semaphore_signal(barrier, inc=1, device_id=(1 - slab, row, col), device_id_type=pl.DeviceIdType.MESH)

    lanes8, lanes16 = low_lanes((8, 128)), low_lanes((16, 128))
    zero = jnp.zeros((1, 64), F32)

    def halves(ref):
        return ref[0:1, 0:128], jnp.concatenate([ref[0:1, 128:192], zero], 1)

    order_channels(order)
    for load in loads[:3]:
        load.wait()

    def spread(t, _):
        for f in range(2):
            natural[t, f] = cin[f, t].astype(F32)
            natural[t, 6 + f] = cmid[f, t].astype(F32)
        for f in range(4):
            natural[t, 2 + f] = video[f, t].astype(F32)
        return 0

    lax.fori_loop(0, 24, spread, 0, unroll=4)
    flat = natural.reshape(24 * 64, 128)
    gain_a, gain_b = halves(gain_in)
    sub = lax.broadcasted_iota(jnp.int32, (8, 128), 0)
    moving = (sub >= 2) & (sub < 6)

    def activate_row(i, _):
        for j in range(8):
            t0, t1, t2 = (flat[pl.ds((3 * j + k) * 64 + i, 8, stride=8)] for k in range(3))
            t1s, t2s = swap(t1), swap(t2)
            pixels = [(t0, t1), (jnp.where(lanes8, t1s, t2s), t2s)]
            done = []
            for a, b in pixels:
                ya, yb = act(a, b, gain_a, gain_b, lanes8)
                done.append((jnp.where(moving, ya, a), jnp.where(moving, yb, b)))
            start = pl.multiple_of(i * 128 + j * 16, 16)
            mixed[pl.ds(start, 16), 0:128] = jnp.concatenate([done[0][0], done[1][0]], 0).astype(BF16)
            mixed[pl.ds(start, 16), 128:256] = jnp.concatenate([done[0][1], done[1][1]], 0).astype(BF16)
        return 0

    lax.fori_loop(0, 8, activate_row, 0)

    def place_rows(u, _):
        start = pl.multiple_of(u * 256, 256)
        ordered = jnp.dot(mixed[pl.ds(start, 256), :], order[...], preferred_element_type=F32)
        for r in range(2):
            at = pl.multiple_of(((2 * u + r + 2) * PITCH + 2) * 8, 8)
            sa[pl.ds(at, 128), :] = ordered[r * 128 : r * 128 + 128, 0:128]
            sb[pl.ds(at, 128), :] = ordered[r * 128 : r * 128 + 128, 128:256]
        small = ordered.astype(BF16)
        for v in range(8):
            top, low = small[v * 16 : v * 16 + 16], small[128 + v * 16 : 128 + v * 16 + 16]
            units[u + 1, v + 1, 0] = top[:, 0:128]
            units[u + 1, v + 1, 1] = low[:, 0:128]
            units[u + 1, v + 1, 2] = jnp.where(lanes16, top[:, 128:256], low[:, 128:256])
        return 0

    lax.fori_loop(0, 4, place_rows, 0)

    pl.semaphore_wait(barrier, 9)

    def span(step, count, away):
        if step == 0:
            return pl.ds(1, count)
        near, far = (1, count + 1) if step < 0 else (count, 0)
        return pl.ds(far if away else near, 1)

    copies = []
    for n, (dr, dc) in enumerate(AROUND):
        copies.append(pltpu.make_async_remote_copy(
            src_ref=units.at[span(dr, 4, False), span(dc, 8, False)],
            dst_ref=units.at[span(dr, 4, True), span(dc, 8, True)],
            send_sem=send_sem.at[n], recv_sem=recv_sem.at[n],
            device_id=neighbour(dr, dc), device_id_type=pl.DeviceIdType.MESH))
    for copy in copies:
        copy.start()

    loads[3].wait()
    lay_out_weights(raw_in, wide, w_in)
    loads[4].wait()
    lay_out_weights(raw_mid, wide, w_mid)

    for copy in copies:
        copy.wait()

    inside_up, inside_down = (row > 0).astype(F32), (row < n_row - 1).astype(F32)
    inside_left, inside_right = (col > 0).astype(F32), (col < n_col - 1).astype(F32)

    def place_unit(u, v, keep):
        at = pl.multiple_of((2 * u * PITCH + 2 * v) * 8, 8)
        sa[pl.ds(at, 16), :] = units[u, v, 0].astype(F32) * keep
        sa[pl.ds(at + PITCH * 8, 16), :] = units[u, v, 1].astype(F32) * keep
        b = units[u, v, 2].astype(F32) * keep
        other = swap(b)
        sb[pl.ds(at, 16), :] = jnp.where(lanes16, b, other)
        sb[pl.ds(at + PITCH * 8, 16), :] = jnp.where(lanes16, other, b)

    for v in range(10):
        side = inside_left if v == 0 else inside_right if v == 9 else 1.0
        place_unit(0, v, inside_up * side)
        place_unit(5, v, inside_down * side)
    for u in range(1, 5):
        place_unit(u, 0, inside_left)
        place_unit(u, 9, inside_right)

    early_copies = [pltpu.make_async_remote_copy(
        src_ref=e, dst_ref=e, send_sem=early_send.at[n], recv_sem=early_recv.at[n],
        device_id=(1 - slab, row, col), device_id_type=pl.DeviceIdType.MESH) for n, e in enumerate((early_in, early_mid))]

    @pl.when(slab == 0)
    def _():
        pack_early(sa, sb, early_in, EARLY_IN)
        early_copies[0].start()

    def place_cache(i, _):
        source = pl.multiple_of(((i + 1) * PITCH + 1) * 8, 8)
        at = pl.multiple_of(i * (PITCH * 8), 8)
        for s, s2 in ((sa, s2a), (sb, s2b)):
            s2[pl.ds(at, COLS_MID * 8), :] = s[pl.ds(source + 6, COLS_MID * 8), :]
        return 0

    lax.fori_loop(0, ROWS_MID, place_cache, 0)

    gather_taps(sa, sb, ta, tb, zp, zq, 2, 5, 9, 7, 11)
    total[...] = convolve(ta, zp, zq, w_in, [2], 5, 9)

    @pl.when(slab == 1)
    def _():
        early_copies[0].wait_recv()
        unpack_early(sa, sb, early_in, EARLY_IN)

    for a in range(2):
        gather_taps(sa, sb, ta, tb, zp, zq, a, 5, 9, 7, 11)
    total[...] += convolve(ta, zp, zq, w_in, [0, 1], 5, 9)

    bias_a, bias_b = halves(bias_in)
    gain_a, gain_b = halves(gain_mid)
    subs16 = lax.broadcasted_iota(jnp.int32, (16, 128), 0)
    left_subs = (subs16 & 4) == 0

    def activate_middle(i, _):
        keep_rows = jnp.where(
            subs16 < 8,
            jnp.where(i == 0, inside_up, 1.0),
            jnp.where(i == 4, inside_down, 1.0))
        for j in range(9):
            start = pl.multiple_of(i * 144 + j * 16, 16)
            a = total[pl.ds(start, 16), 0:128] + bias_a
            b = total[pl.ds(start, 16), 128:256] + bias_b
            ya, yb = act(a, b, gain_a, gain_b, lanes16)
            keep = keep_rows
            if j == 0:
                keep = jnp.where(left_subs, keep * inside_left, keep)
            if j == 8:
                keep = jnp.where(left_subs, keep, keep * inside_right)
            mixed[pl.ds(start, 16), 0:128] = (ya * keep).astype(BF16)
            mixed[pl.ds(start, 16), 128:256] = (yb * keep).astype(BF16)
        return 0

    lax.fori_loop(0, 5, activate_middle, 0)

    def place_middle(i, _):
        start = pl.multiple_of(i * 144, 16)
        ordered = jnp.dot(mixed[pl.ds(start, 144), :], order[...], preferred_element_type=F32)
        at = pl.multiple_of(i * (PITCH * 8), 8)
        for j in range(9):
            for n, step in enumerate((0, 9, 5 * PITCH, 5 * PITCH + 9)):
                y = ordered[j * 16 + 4 * n : j * 16 + 4 * n + 4]
                s2a[pl.ds(at + (j + step) * 8 + 2, 4), :] = y[:, 0:128]
                s2b[pl.ds(at + (j + step) * 8 + 2, 4), :] = y[:, 128:256]
        return 0

    lax.fori_loop(0, 5, place_middle, 0)

    @pl.when(slab == 0)
    def _():
        pack_early(s2a, s2b, early_mid, EARLY_MID)
        early_copies[1].start()

    gather_taps(s2a, s2b, ta, tb, zp, zq, 2, 4, 8, 6, 10)
    total[0:512] = convolve(ta, zp, zq, w_mid, [2], 4, 8)

    @pl.when(slab == 1)
    def _():
        early_copies[1].wait_recv()
        unpack_early(s2a, s2b, early_mid, EARLY_MID)

    for a in range(2):
        gather_taps(s2a, s2b, ta, tb, zp, zq, a, 4, 8, 6, 10)
    total[0:512] += convolve(ta, zp, zq, w_mid, [0, 1], 4, 8)

    bias_a, bias_b = halves(bias_mid)

    def restore(i, _):
        for j in range(4):
            start = pl.multiple_of(i * 128 + j * 32, 32)
            for h in range(2):
                even, odd = start + 8 * h, start + 16 + 8 * h
                ae = total[pl.ds(even, 8), 0:128] + bias_a
                be = total[pl.ds(even, 8), 128:256] + bias_b
                ao = swap(total[pl.ds(odd, 8), 0:128] + bias_a)
                bo = swap(total[pl.ds(odd, 8), 128:256] + bias_b)
                natural[3 * j, i + 4 * h] = ae
                natural[3 * j + 1, i + 4 * h] = jnp.where(lanes8, be, ao)
                natural[3 * j + 2, i + 4 * h] = jnp.where(lanes8, ao, bo)
        return 0

    lax.fori_loop(0, 4, restore, 0)

    def finish(t, _):
        start = pl.multiple_of(t * 64, 64)
        for h in range(2):
            for f in range(4):
                branch = flat[pl.ds(start + 4 * h + f, 8, stride=8)]
                out[f, t + 12 * h] = (video[f, t + 12 * h].astype(F32) + branch).astype(BF16)
        return 0

    lax.fori_loop(0, 12, finish, 0, unroll=4)

    @pl.when(slab == 0)
    def _():
        early_copies[0].wait_send()
        early_copies[1].wait_send()


def body(sizes, video, cache_in, cache_mid, gain_in, gain_mid, conv_in, bias_in, conv_mid, bias_mid):
    def tiles(x):
        return x.reshape(x.shape[0], 8, 24, 128).transpose(0, 2, 1, 3)

    def taps(x):
        return x.reshape(3, 3, 864, 128).transpose(0, 2, 1, 3)

    def line(x):
        return x.reshape(1, CHAN)

    hbm, vmem = pl.BlockSpec(memory_space=pl.ANY), pl.BlockSpec(memory_space=pltpu.VMEM)
    scratch = [
        pltpu.VMEM((4, 24, 8, 128), BF16),
        pltpu.VMEM((2, 24, 8, 128), BF16),
        pltpu.VMEM((2, 24, 8, 128), BF16),
        pltpu.VMEM((3, 864, 3, 128), BF16),
        pltpu.VMEM((3, 864, 3, 128), BF16),
        pltpu.VMEM((3, 14 * 128, 256), BF16),
        pltpu.VMEM((3, 14 * 128, 256), BF16),
        pltpu.VMEM((4 * 24, 8, 128), F32),
        pltpu.VMEM((24, 8, 8, 128), F32),
        pltpu.VMEM((1024, 256), BF16),
        pltpu.VMEM((256, 256), BF16),
        pltpu.VMEM((ROWS_IN * PITCH * 8, 128), F32),
        pltpu.VMEM((ROWS_IN * PITCH * 8, 128), F32),
        pltpu.VMEM((EARLY_MID * 64, 128), F32),
        pltpu.VMEM((EARLY_MID * 64, 128), F32),
        pltpu.VMEM((6, 10, 3, 16, 128), BF16),
        pltpu.VMEM((EARLY_IN * 3 // 2, 16, 128), BF16),
        pltpu.VMEM((EARLY_MID * 3 // 2, 16, 128), BF16),
        pltpu.VMEM((3, 7, 11, 16, 128), BF16),
        pltpu.VMEM((3, 7, 11, 16, 128), BF16),
        pltpu.VMEM((3, 5, 11, 16, 128), BF16),
        pltpu.VMEM((3, 5, 10, 16, 128), BF16),
        pltpu.VMEM((720, 256), F32),
        pltpu.SemaphoreType.DMA((5,)),
        pltpu.SemaphoreType.DMA((8,)),
        pltpu.SemaphoreType.DMA((8,)),
        pltpu.SemaphoreType.DMA((2,)),
        pltpu.SemaphoreType.DMA((2,)),
    ]
    result = pl.pallas_call(
        functools.partial(kernel, sizes),
        out_shape=jax.ShapeDtypeStruct((4, 24, 8, 128), BF16),
        in_specs=[hbm, hbm, hbm, vmem, vmem, hbm, vmem, hbm, vmem],
        out_specs=vmem,
        scratch_shapes=scratch,
        compiler_params=pltpu.CompilerParams(
            collective_id=0, has_side_effects=True, vmem_limit_bytes=48 << 20),
        cost_estimate=pl.CostEstimate(flops=3_000_000_000, bytes_accessed=6_000_000, transcendentals=300_000),
    )(tiles(video), tiles(cache_in), tiles(cache_mid), line(gain_in), line(gain_mid),
      taps(conv_in), line(bias_in), taps(conv_mid), line(bias_mid))
    return result.transpose(0, 2, 1, 3).reshape(video.shape)


def solution(mesh):
    tile = P("slab", "row", "col")
    cache = P(None, "row", "col")
    sizes = (mesh.shape["row"], mesh.shape["col"])
    return jax.shard_map(
        functools.partial(body, sizes), mesh=mesh,
        in_specs=(tile, cache, cache, P(), P(), P(), P(), P(), P()),
        out_specs=tile, check_vma=False)
```

time: 159 us -> 45.1 us (0.28)
  the two profiles are of different devices: /device:TPU:70 before, /device:TPU:1 now
where the time goes in v1:
time: 45.1 us; the launch traced here: 44.7 us
  Pallas kernels  35.1 us (78%)
  local copies, waits for them, and re-layouts  9.6 us (21%)
    pallas_call x1, Pallas kernels, body(): pl.pallas_call(functools.partial(kernel, sizes), out_shape=jax.ShapeDtype...  35.1 us
    unnamed x19, local copies, waits for them, and re-layouts  9.6 us

profile of v1, /device:TPU:1, one launch (start us, length us, event | category | flops | bytes accessed | tf_op | source)
XLA Modules:
  0.0 44.7 jit_solution(7225870330552188638)
XLA Ops:
  0.0 0.0 copy-start
  0.0 1.7 %copy-done = bf16[3,3,110592]{2,1,0:T(4,128)(2,1)S(1)} copy-done((bf16[3,3,110592]{2,1,0:T(4,128)(2,1)S(1)}, bf16[3,3,110592]{2,1,0:T(4,128)(2,1)}, u32[]{:S(2)}) %copy-start) | copy-done | bytes 1990680
  1.8 0.0 copy-start.1
  1.8 1.7 %copy-done.1 = bf16[3,3,110592]{2,1,0:T(4,128)(2,1)S(1)} copy-done((bf16[3,3,110592]{2,1,0:T(4,128)(2,1)S(1)}, bf16[3,3,110592]{2,1,0:T(4,128)(2,1)}, u32[]{:S(2)}) %copy-start.1) | copy-done | bytes 1990680
  3.5 0.0 copy-start.2
  3.5 0.9 %copy-done.2 = bf16[4,8,3072]{2,1,0:T(8,128)(2,1)S(1)} copy-done((bf16[4,8,3072]{2,1,0:T(8,128)(2,1)S(1)}, bf16[4,8,3072]{2,1,0:T(8,128)(2,1)}, u32[]{:S(2)}) %copy-start.2) | copy-done | bytes 196632
  4.4 0.0 copy-start.3
  4.4 0.9 %copy-done.3 = bf16[2,8,3072]{2,1,0:T(8,128)(2,1)S(1)} copy-done((bf16[2,8,3072]{2,1,0:T(8,128)(2,1)S(1)}, bf16[2,8,3072]{2,1,0:T(8,128)(2,1)}, u32[]{:S(2)}) %copy-start.3) | copy-done | bytes 98328
  5.3 0.0 copy-start.4
  5.3 0.9 %copy-done.4 = bf16[2,8,3072]{2,1,0:T(8,128)(2,1)S(1)} copy-done((bf16[2,8,3072]{2,1,0:T(8,128)(2,1)S(1)}, bf16[2,8,3072]{2,1,0:T(8,128)(2,1)}, u32[]{:S(2)}) %copy-start.4) | copy-done | bytes 98328
  6.2 0.0 copy-start.5
  6.2 0.7 %copy-done.5 = f32[192]{0:T(256)S(1)} copy-done((f32[192]{0:T(256)S(1)}, f32[192]{0:T(256)}, u32[]{:S(2)}) %copy-start.5) | copy-done | bytes 792
  6.9 0.0 copy-start.6
  6.9 0.7 %copy-done.6 = f32[192]{0:T(256)S(1)} copy-done((f32[192]{0:T(256)S(1)}, f32[192]{0:T(256)}, u32[]{:S(2)}) %copy-start.6) | copy-done | bytes 792
  7.6 0.0 copy-start.7
  7.6 0.7 %copy-done.7 = f32[192]{0:T(256)S(1)} copy-done((f32[192]{0:T(256)S(1)}, f32[192]{0:T(256)}, u32[]{:S(2)}) %copy-start.7) | copy-done | bytes 792
  8.3 0.0 copy-start.8
  8.3 0.7 %copy-done.8 = f32[192]{0:T(256)S(1)} copy-done((f32[192]{0:T(256)S(1)}, f32[192]{0:T(256)}, u32[]{:S(2)}) %copy-start.8) | copy-done | bytes 792
  8.9 35.1 %shard_map.91 = bf16[4,24,8,128]{3,2,1,0:T(8,128)(2,1)S(1)} custom-call(bf16[4,24,8,128]{3,2,1,0:T(8,128)(2,1)S(1)} %bitcast.25, bf16[2,24,8,128]{3,2,1,0:T(8,128)(2,1)S(1)} %bitcast.26, bf16[2,24,8,128]{3,2,1,0:T(8,128)(2,1)S(1)} %bitcast.27, f32[1,192]{1,0:T(1,128)S(1)} %bitcast.28, f32[1,192]{1,0:T(1,128)S(1)} %bitcast.29, ...), custom_call_target="tpu_custom_call" | custom-call | flops 3000000000 | bytes 6000000 | tf_op jit(solution)/shard_map/pallas_call | solution.py:441
  44.1 0.7 %copy.11 = bf16[4,8,3072]{2,1,0:T(8,128)(2,1)} copy(bf16[4,8,3072]{2,1,0:T(8,128)(2,1)S(1)} %bitcast.22) | data formatting | bytes 393216
Async XLA Ops:
  0.0 1.7 %copy-start = (bf16[3,3,110592]{2,1,0:T(4,128)(2,1)S(1)}, bf16[3,3,110592]{2,1,0:T(4,128)(2,1)}, u32[]{:S(2)}) copy-start(bf16[3,3,110592]{2,1,0:T(4,128)(2,1)} %param.14) | copy-start | bytes 5971972
  1.8 1.7 %copy-start.1 = (bf16[3,3,110592]{2,1,0:T(4,128)(2,1)S(1)}, bf16[3,3,110592]{2,1,0:T(4,128)(2,1)}, u32[]{:S(2)}) copy-start(bf16[3,3,110592]{2,1,0:T(4,128)(2,1)} %param.16) | copy-start | bytes 5971972
  3.5 0.9 %copy-start.2 = (bf16[4,8,3072]{2,1,0:T(8,128)(2,1)S(1)}, bf16[4,8,3072]{2,1,0:T(8,128)(2,1)}, u32[]{:S(2)}) copy-start(bf16[4,8,3072]{2,1,0:T(8,128)(2,1)} %param.9) | copy-start | bytes 589828
  4.4 0.9 %copy-start.3 = (bf16[2,8,3072]{2,1,0:T(8,128)(2,1)S(1)}, bf16[2,8,3072]{2,1,0:T(8,128)(2,1)}, u32[]{:S(2)}) copy-start(bf16[2,8,3072]{2,1,0:T(8,128)(2,1)} %param.10) | copy-start | bytes 294916
  5.3 0.9 %copy-start.4 = (bf16[2,8,3072]{2,1,0:T(8,128)(2,1)S(1)}, bf16[2,8,3072]{2,1,0:T(8,128)(2,1)}, u32[]{:S(2)}) copy-start(bf16[2,8,3072]{2,1,0:T(8,128)(2,1)} %param.11) | copy-start | bytes 294916
  6.2 0.7 %copy-start.5 = (f32[192]{0:T(256)S(1)}, f32[192]{0:T(256)}, u32[]{:S(2)}) copy-start(f32[192]{0:T(256)} %param.12) | copy-start | bytes 2308
  6.9 0.7 %copy-start.6 = (f32[192]{0:T(256)S(1)}, f32[192]{0:T(256)}, u32[]{:S(2)}) copy-start(f32[192]{0:T(256)} %param.13) | copy-start | bytes 2308
  7.6 0.7 %copy-start.7 = (f32[192]{0:T(256)S(1)}, f32[192]{0:T(256)}, u32[]{:S(2)}) copy-start(f32[192]{0:T(256)} %param.15) | copy-start | bytes 2308
  8.3 0.7 %copy-start.8 = (f32[192]{0:T(256)S(1)}, f32[192]{0:T(256)}, u32[]{:S(2)}) copy-start(f32[192]{0:T(256)} %param.17) | copy-start | bytes 2308

commit v2 on v0

v2 whole, which is shorter than its diff:
```python
import functools

import jax
import jax.numpy as jnp
from jax import lax
from jax.experimental import pallas as pl
from jax.experimental.pallas import tpu as pltpu
from jax.sharding import PartitionSpec as P

F32 = jnp.float32
BF16 = jnp.bfloat16
CHAN = 192
HALF = 20
LINE = 2 * HALF
PAD = 3
IMAGE = 13 * LINE
MIDDLE = 5 * LINE
AROUND = [(-1, 0), (1, 0), (0, -1), (0, 1), (-1, -1), (-1, 1), (1, -1), (1, 1)]


def low_lanes(shape):
    return lax.broadcasted_iota(jnp.int32, shape, len(shape) - 1) < 64


def swap(x):
    return pltpu.roll(x, 64, 1)


def act(a, b, gain_a, gain_b, lanes):
    square = a * a + jnp.where(lanes, b * b, 0.0)
    mean = jnp.sum(square, axis=1, keepdims=True) * (1.0 / CHAN)
    scale = lax.rsqrt(mean + 1e-6)
    ua, ub = a * scale * gain_a, b * scale * gain_b
    return ua / (1.0 + jnp.exp(-ua)), ub / (1.0 + jnp.exp(-ub))


def order_channels(order):
    c = lax.broadcasted_iota(jnp.int32, (256, 256), 0)
    o = lax.broadcasted_iota(jnp.int32, (256, 256), 1)
    o = jnp.where(o < CHAN, o, o - 64)
    r = o & 15
    source = (o - r) + jnp.where(r < 8, 2 * r, 2 * r - 15)
    order[...] = jnp.where(c == source, 1.0, 0.0).astype(BF16)


def lay_out_weights(raw, wide, out):
    per = wide.shape[0] // 24
    lanes = low_lanes((8, 128))
    flat = wide.reshape(wide.shape[0] * 8, 128)
    out[:, 13 * 128 : 13 * 128 + 64, :] = jnp.zeros((3, 64, 256), BF16)

    def step(n, _):
        a, part = n // (36 // per), n % (36 // per)
        for u in range(per):
            g = part * per + u
            wide[pl.ds(u * 24, 24), 0:3, :] = raw[a, pl.ds(g * 24, 24)].astype(F32)
            q, group = g // 12, g % 12
            for p in range(3):
                first = flat[pl.ds(u * 192 + p, 8, stride=24)]
                both = flat[pl.ds(u * 192 + 8 + p, 8, stride=24)]
                second = swap(flat[pl.ds(u * 192 + 16 + p, 8, stride=24)])
                odd = jnp.where(lanes, swap(both), second)
                row_a = (p * 3 + q) * 128 + 16 * group
                row_b = (9 + q) * 128 + 64 * p if p < 2 else 12 * 128 + 64 * q + jnp.where(q == 2, 64, 0)
                row = jnp.where(group < 8, row_a, row_b + 16 * (group - 8))
                row = pl.multiple_of(row, 16)
                out[a, pl.ds(row, 16), 0:128] = jnp.concatenate([first, odd], 0).astype(BF16)
                out[a, pl.ds(row, 16), 128:256] = jnp.concatenate([both, second], 0).astype(BF16)
        return 0

    lax.fori_loop(0, 3 * 36 // per, step, 0)


def split_columns(t0, t1, t2, lanes):
    t1s, t2s = swap(t1), swap(t2)
    return [(t0, t1), (jnp.where(lanes, t1s, t2s), t2s)]


def gather_taps(sa, sb, ta, tb, start_of, step, apart, pairs, rows, cols):
    size = start_of(1, 0, 0) - start_of(0, 0, 0)

    def tile(s, at):
        first = s[pl.ds(at, 8, stride=step), :]
        second = s[pl.ds(at + apart * size, 8, stride=step), :]
        return jnp.concatenate([first, second], 0).astype(BF16)

    def body(n, _):
        g, i = n // rows, n % rows
        for j in range(cols):
            at = start_of(g, i, j)
            ta[g, i, j] = tile(sa, at)
            tb[g, i, j] = tile(sb, at)
        return 0

    lax.fori_loop(0, pairs * rows, body, 0)


def merge_taps(tb, zp, zq, pairs, rows, cols):
    lanes = low_lanes((16, 128))

    def body(n, _):
        g, i = n // rows, n % rows
        for j in range(cols):
            zp[g, i, j] = jnp.where(lanes, tb[g, i, j], tb[g, i + 1, j])
        for j in range(cols - 1):
            zq[g, i, j] = jnp.where(lanes, tb[g, i + 2, j], tb[g, i + 2, j + 1])
        return 0

    lax.fori_loop(0, pairs * rows, body, 0)


def convolve(ta, zp, zq, weights, pairs, rows, cols):
    columns = []
    for a in range(3):
        g = slice(a, a + pairs)
        columns += [ta[g, p : p + rows, q : q + cols] for p in range(3) for q in range(3)]
        columns += [zp[g, :, q : q + cols] for q in range(3)]
        columns += [zq[g, :, q : q + cols] for q in range(2)]
    columns = [x.reshape(pairs * rows * cols * 16, 128) for x in columns]
    weight = weights[...].reshape(3 * 14 * 128, 256)
    return jnp.dot(jnp.concatenate(columns, 1), weight, preferred_element_type=F32)


def kernel(sizes, video_hbm, cin_hbm, cmid_hbm, gin_hbm, gmid_hbm, win_hbm, bin_hbm, wmid_hbm, bmid_hbm, out,
           gain_in, gain_mid, bias_in, bias_mid, video, cin, cmid, raw_in, raw_mid, w_in, w_mid, wide, mixed, order,
           oa, ob, corner, sa, sb, ma, mb, tile, side, angle, got_tile, got_row, got_side, got_angle,
           ta, tb, zp, zq, ua, ub, vp, vq, total_a, total_b,
           load_sem, send_sem, recv_sem, tile_sem):
    n_row, n_col = sizes
    slab, row, col = lax.axis_index("slab"), lax.axis_index("row"), lax.axis_index("col")
    loads = [pltpu.make_async_copy(src, dst, load_sem.at[n]) for n, (src, dst) in enumerate(
        [(video_hbm, video), (cin_hbm, cin), (cmid_hbm, cmid), (gin_hbm, gain_in), (gmid_hbm, gain_mid),
         (bin_hbm, bias_in), (bmid_hbm, bias_mid), (win_hbm, raw_in), (wmid_hbm, raw_mid)])]
    for load in loads:
        load.start()

    up, down, left, right = row > 0, row < n_row - 1, col > 0, col < n_col - 1
    there = [up, down, left, right, up & left, up & right, down & left, down & right]

    def device(s, dr, dc):
        return (s, lax.rem(row + dr + n_row, n_row), lax.rem(col + dc + n_col, n_col))

    barrier = pltpu.get_barrier_semaphore()
    for s in range(2):
        for (dr, dc), has in zip(AROUND, there):
            @pl.when(has)
            def _():
                pl.semaphore_signal(barrier, inc=1, device_id=device(s, dr, dc), device_id_type=pl.DeviceIdType.MESH)
    pl.semaphore_signal(barrier, inc=1, device_id=(1 - slab, row, col), device_id_type=pl.DeviceIdType.MESH)
    n_up_down, n_sides = up.astype(jnp.int32) + down.astype(jnp.int32), left.astype(jnp.int32) + right.astype(jnp.int32)
    greetings = 2 * (n_up_down + n_sides + n_up_down * n_sides) + 1

    lanes8, lanes16 = low_lanes((8, 128)), low_lanes((16, 128))
    zero = jnp.zeros((1, 64), F32)

    def halves(ref):
        return ref[0:1, 0:128], jnp.concatenate([ref[0:1, 128:192], zero], 1)

    order_channels(order)
    for load in loads[:7]:
        load.wait()

    def columns_of(ref, f, j):
        return split_columns(*(ref[f, 3 * j + k].astype(F32) for k in range(3)), lanes8)

    def put_mixed(f, j, pixels):
        start = pl.multiple_of(f * 128 + j * 16, 16)
        mixed[pl.ds(start, 16), 0:128] = jnp.concatenate([pixels[0][0], pixels[1][0]], 0).astype(BF16)
        mixed[pl.ds(start, 16), 128:256] = jnp.concatenate([pixels[0][1], pixels[1][1]], 0).astype(BF16)

    gain_a, gain_b = halves(gain_in)

    def activate_frame(n, _):
        f = n // 2
        for k in range(4):
            j = (n % 2) * 4 + k
            put_mixed(f, j, [act(a, b, gain_a, gain_b, lanes8) for a, b in columns_of(video, f, j)])
        return 0

    def mix_caches(j, _):
        for f in range(2):
            put_mixed(f, j, columns_of(cmid, f, j))
            put_mixed(2 + f, j, columns_of(cin, f, j))
        return 0

    def reorder():
        ordered = jnp.dot(mixed[0:512], order[...], preferred_element_type=F32)
        oa[...] = ordered[:, 0:128]
        ob[...] = ordered[:, 128:256]

    def line_of(o, f, i):
        return [o[pl.ds(f * 128 + h * 64 + i, 8, stride=8), :] for h in range(2)]

    def pack(k):
        def two_rows(n, _):
            f, u = n // 4, n % 4
            for r in range(2):
                tile[k, f, u, r] = jnp.concatenate(line_of(oa, f, 2 * u + r), 0).astype(BF16)
            b = [jnp.concatenate(line_of(ob, f, 2 * u + r), 0) for r in range(2)]
            tile[k, f, u, 2] = jnp.where(lanes16, b[0], b[1]).astype(BF16)
            return 0

        lax.fori_loop(0, 16, two_rows, 0, unroll=4)
        for v, j in enumerate((0, 14)):
            for f in range(4):
                side[k, v, f // 2, f % 2] = oa[pl.ds((f * 16 + j) * 8, 16), :].astype(BF16)
            for f in range(0, 4, 2):
                b = [ob[pl.ds(((f + e) * 16 + j) * 8, 16), :] for e in range(2)]
                side[k, v, f // 2, 2] = jnp.where(lanes16, b[0], b[1]).astype(BF16)
        for n, (i0, j0) in enumerate(((0, 0), (0, 14), (6, 0), (6, 14))):
            for h, o in enumerate((oa, ob)):
                for x in range(4):
                    at = (j0 + x % 2) * 8 + i0 + x // 2
                    corner[2 * n + h, 4 * x : 4 * x + 4, :] = o[pl.ds(at, 4, stride=128), :]
        for n in range(4):
            for h in range(2):
                angle[k, n, h] = corner[2 * n + h].astype(BF16)

    def messages(k, s, slot):
        sources = [tile.at[k, :, 0], tile.at[k, :, 3], side.at[k, 0], side.at[k, 1]] + [angle.at[k, n] for n in range(4)]
        targets = [got_row.at[slot, 1], got_row.at[slot, 0], got_side.at[slot, 1], got_side.at[slot, 0]]
        targets += [got_angle.at[slot, 3 - n] for n in range(4)]
        return [pltpu.make_async_remote_copy(
            src_ref=src, dst_ref=dst, send_sem=send_sem.at[slot, n], recv_sem=recv_sem.at[slot, n],
            device_id=device(s, dr, dc), device_id_type=pl.DeviceIdType.MESH)
            for n, (src, dst, (dr, dc)) in enumerate(zip(sources, targets, AROUND))]

    def each(copies, method, condition=None):
        exist = [there[n] for n in (1, 0, 3, 2, 7, 6, 5, 4)] if method == "wait_recv" else there
        for copy, has in zip(copies, exist):
            @pl.when(has if condition is None else has & condition)
            def _():
                getattr(copy, method)()

    own = messages(0, slab, 1)
    early_frames = messages(0, 1, 0)
    early_caches = messages(1, 0, 0)
    to_partner = pltpu.make_async_remote_copy(
        src_ref=tile.at[0], dst_ref=got_tile, send_sem=tile_sem.at[0], recv_sem=tile_sem.at[1],
        device_id=(1 - slab, row, col), device_id_type=pl.DeviceIdType.MESH)

    def place_tile(f0):
        def one(f, i, line, r):
            at = ((f0 + f) * 13 + line + PAD) * LINE + r * HALF + 2
            for o, s in ((oa, sa), (ob, sb)):
                for h, x in enumerate(line_of(o, f, i)):
                    s[pl.ds(at + 8 * h, 8), :] = x

        def frame(f, _):
            for i in range(8):
                if i < 5:
                    one(f, i, i + 2, 0)
                if i > 2:
                    one(f, i, i - 3, 1)
            return 0

        lax.fori_loop(0, 4, frame, 0)

    lax.fori_loop(0, 8, activate_frame, 0)
    reorder()
    pack(0)
    pl.semaphore_wait(barrier, greetings)
    each(own, "start")
    each(early_frames, "start", slab == 0)

    @pl.when(slab == 0)
    def _():
        to_partner.start()

    place_tile(4)
    lax.fori_loop(0, 8, mix_caches, 0)
    reorder()

    @pl.when(slab == 1)
    def _():
        pack(1)

    each(early_caches, "start", slab == 1)

    @pl.when(slab == 0)
    def _():
        place_tile(0)

    loads[7].wait()
    lay_out_weights(raw_in, wide, w_in)
    loads[8].wait()
    lay_out_weights(raw_mid, wide, w_mid)

    def clear(x, has):
        return jnp.where(has, x, 0.0)

    def unmerge(b):
        other = swap(b)
        return jnp.where(lanes16, b, other), jnp.where(lanes16, other, b)

    def place_rows(slot):
        for v, has in enumerate((up, down)):
            line, r = ((0, 0), (5, 1))[v]

            def frame(f, _):
                at = ((slot * 4 + f) * 13 + line + PAD) * LINE + r * HALF + 2
                b = unmerge(clear(got_row[slot, v, f, 2].astype(F32), has))
                for n in range(2):
                    sa[pl.ds(at + n * LINE, 16), :] = clear(got_row[slot, v, f, n].astype(F32), has)
                    sb[pl.ds(at + n * LINE, 16), :] = b[n]
                return 0

            lax.fori_loop(0, 4, frame, 0, unroll=True)

    def put_columns(s, f, j, x):
        for n in range(2):
            at = f * IMAGE + j + n
            s[pl.ds(at + (2 + PAD) * LINE, 8, stride=LINE), :] = x[8 * n : 8 * n + 8]
            s[pl.ds(at + (PAD - 3) * LINE + HALF, 8, stride=LINE), :] = x[8 * n : 8 * n + 8]

    def place_sides(slot):
        for v, has in enumerate((left, right)):
            for pair in range(2):
                b = unmerge(clear(got_side[slot, v, pair, 2].astype(F32), has))
                for e in range(2):
                    f = slot * 4 + pair * 2 + e
                    put_columns(sa, f, 18 * v, clear(got_side[slot, v, pair, e].astype(F32), has))
                    put_columns(sb, f, 18 * v, b[e])

    def place_angles(slot):
        for n, has in enumerate(there[4:]):
            for h, s in enumerate((sa, sb)):
                corner[2 * n + h] = clear(got_angle[slot, n, h].astype(F32), has)
        for n in range(4):
            line, r = ((0, 0), (5, 1))[n // 2]
            for h, s in enumerate((sa, sb)):
                for x in range(4):
                    at = slot * 4 * IMAGE + (line + x // 2 + PAD) * LINE + r * HALF + 18 * (n % 2) + x % 2
                    s[pl.ds(at, 4, stride=IMAGE), :] = corner[2 * n + h, 4 * x : 4 * x + 4, :]

    def unpack_tile():
        def frame(f, _):
            for u in range(4):
                b = unmerge(got_tile[f, u, 2].astype(F32))
                for n in range(2):
                    i = 2 * u + n
                    a = got_tile[f, u, n].astype(F32)
                    for line, r, fits in ((i + 2, 0, i < 5), (i - 3, 1, i > 2)):
                        if fits:
                            at = (f * 13 + line + PAD) * LINE + r * HALF + 2
                            sa[pl.ds(at, 16), :] = a
                            sb[pl.ds(at, 16), :] = b[n]
            return 0

        lax.fori_loop(0, 4, frame, 0)

    @pl.when(slab == 1)
    def _():
        to_partner.wait_recv()
        unpack_tile()

    each(own, "wait_recv")
    for slot in (1, 0):
        if slot == 0:
            each(early_frames, "wait_recv")
        place_rows(slot)
        place_sides(slot)
        place_angles(slot)

    def start_in(g, i, j):
        return (g * 13 + i + PAD) * LINE + j

    gather_taps(sa, sb, ta, tb, start_in, 5, 3, 5, 7, 7)
    merge_taps(tb, zp, zq, 5, 5, 7)
    result = convolve(ta, zp, zq, w_in, 3, 5, 5)
    total_a[...] = result[:, 0:128]
    total_b[...] = result[:, 128:256]

    bias_a, bias_b = halves(bias_in)
    gain_a, gain_b = halves(gain_mid)
    subs = lax.broadcasted_iota(jnp.int32, (16, 128), 0) & 7
    ones = jnp.ones((16, 128), F32)

    def activate_middle(n, _):
        i = n % 5
        gone = ((i == 0) & jnp.logical_not(up) & (subs < 4)) | ((i == 4) & jnp.logical_not(down) & (subs >= 4))
        keep_rows = jnp.where(gone, 0.0, ones)
        for j in range(5):
            start = pl.multiple_of(n * 80 + j * 16, 16)
            a = total_a[pl.ds(start, 16), :] + bias_a
            b = total_b[pl.ds(start, 16), :] + bias_b
            ya, yb = act(a, b, gain_a, gain_b, lanes16)
            keep = keep_rows
            if j == 0:
                keep = jnp.where(jnp.logical_not(left) & ((subs & 3) == 0), 0.0, keep)
            if j == 2:
                keep = jnp.where(jnp.logical_not(right) & ((subs & 3) == 3), 0.0, keep)
            mixed[pl.ds(start, 16), 0:128] = (ya * keep).astype(BF16)
            mixed[pl.ds(start, 16), 128:256] = (yb * keep).astype(BF16)
        return 0

    lax.fori_loop(0, 15, activate_middle, 0)

    def place_middle(k, _):
        start = pl.multiple_of(k * 400, 16)
        ordered = jnp.dot(mixed[pl.ds(start, 400), :], order[...], preferred_element_type=F32)
        for n in range(25):
            for h in range(2):
                at = (k + 3 * h) * MIDDLE + (n // 5) * LINE + n % 5
                y = ordered[n * 16 + 8 * h : n * 16 + 8 * h + 8]
                ma[pl.ds(at, 8, stride=5), :] = y[:, 0:128]
                mb[pl.ds(at, 8, stride=5), :] = y[:, 128:256]
        return 0

    lax.fori_loop(0, 3, place_middle, 0)

    @pl.when(slab == 0)
    def _():
        def frame(f, _):
            for n in range(10):
                line, r = (n + 1, 0) if n < 6 else (n - 4, 1)
                source = (f * 13 + line + PAD) * LINE + r * HALF + 1
                at = f * MIDDLE + (n % 5) * LINE + (n // 5) * HALF
                for s, m in ((sa, ma), (sb, mb)):
                    m[pl.ds(at, 16), :] = s[pl.ds(source, 16), :]
                    m[pl.ds(at + 16, 2), :] = s[pl.ds(source + 16, 2), :]
            return 0

        lax.fori_loop(0, 2, frame, 0)

    def start_mid(g, i, j):
        return g * MIDDLE + (i % 5) * LINE + (i // 5) * HALF + j

    gather_taps(ma, mb, ua, ub, start_mid, 2, 2, 4, 10, 4)
    merge_taps(ub, vp, vq, 4, 8, 4)
    result = convolve(ua, vp, vq, w_mid, 2, 8, 2)
    total_a[0:512] = result[:, 0:128]
    total_b[0:512] = result[:, 128:256]

    bias_a, bias_b = halves(bias_mid)

    def restore(c, _):
        for f in range(4):
            at = (f % 2) * 256 + (f // 2) * 8 + c
            ae = total_a[pl.ds(at, 8, stride=32), :] + bias_a
            be = total_b[pl.ds(at, 8, stride=32), :] + bias_b
            ao = swap(total_a[pl.ds(at + 16, 8, stride=32), :] + bias_a)
            bo = swap(total_b[pl.ds(at + 16, 8, stride=32), :] + bias_b)
            for k, branch in enumerate((ae, jnp.where(lanes8, be, ao), jnp.where(lanes8, ao, bo))):
                out[f, 3 * c + k] = (video[f, 3 * c + k].astype(F32) + branch).astype(BF16)
        return 0

    lax.fori_loop(0, 8, restore, 0)

    each(own, "wait_send")
    each(early_frames, "wait_send", slab == 0)
    each(early_caches, "wait_send", slab == 1)

    @pl.when(slab == 0)
    def _():
        to_partner.wait_send()


def body(sizes, video, cache_in, cache_mid, gain_in, gain_mid, conv_in, bias_in, conv_mid, bias_mid):
    def tiles(x):
        return x.reshape(x.shape[0], 8, 24, 128).transpose(0, 2, 1, 3)

    def taps(x):
        return x.reshape(3, 3, 864, 128).transpose(0, 2, 1, 3)

    def line(x):
        return x.reshape(1, CHAN)

    hbm, vmem = pl.BlockSpec(memory_space=pltpu.HBM), pl.BlockSpec(memory_space=pltpu.VMEM)
    scratch = [
        pltpu.VMEM((1, CHAN), F32),
        pltpu.VMEM((1, CHAN), F32),
        pltpu.VMEM((1, CHAN), F32),
        pltpu.VMEM((1, CHAN), F32),
        pltpu.VMEM((4, 24, 8, 128), BF16),
        pltpu.VMEM((2, 24, 8, 128), BF16),
        pltpu.VMEM((2, 24, 8, 128), BF16),
        pltpu.VMEM((3, 864, 3, 128), BF16),
        pltpu.VMEM((3, 864, 3, 128), BF16),
        pltpu.VMEM((3, 14 * 128, 256), BF16),
        pltpu.VMEM((3, 14 * 128, 256), BF16),
        pltpu.VMEM((4 * 24, 8, 128), F32),
        pltpu.VMEM((1200, 256), BF16),
        pltpu.VMEM((256, 256), BF16),
        pltpu.VMEM((512, 128), F32),
        pltpu.VMEM((512, 128), F32),
        pltpu.VMEM((8, 16, 128), F32),
        pltpu.VMEM((8 * IMAGE, 128), F32),
        pltpu.VMEM((8 * IMAGE, 128), F32),
        pltpu.VMEM((6 * MIDDLE, 128), F32),
        pltpu.VMEM((6 * MIDDLE, 128), F32),
        pltpu.VMEM((2, 4, 4, 3, 16, 128), BF16),
        pltpu.VMEM((2, 2, 2, 3, 16, 128), BF16),
        pltpu.VMEM((2, 4, 2, 16, 128), BF16),
        pltpu.VMEM((4, 4, 3, 16, 128), BF16),
        pltpu.VMEM((2, 2, 4, 3, 16, 128), BF16),
        pltpu.VMEM((2, 2, 2, 3, 16, 128), BF16),
        pltpu.VMEM((2, 4, 2, 16, 128), BF16),
        pltpu.VMEM((5, 7, 7, 16, 128), BF16),
        pltpu.VMEM((5, 7, 7, 16, 128), BF16),
        pltpu.VMEM((5, 5, 7, 16, 128), BF16),
        pltpu.VMEM((5, 5, 6, 16, 128), BF16),
        pltpu.VMEM((4, 10, 4, 16, 128), BF16),
        pltpu.VMEM((4, 10, 4, 16, 128), BF16),
        pltpu.VMEM((4, 8, 4, 16, 128), BF16),
        pltpu.VMEM((4, 8, 3, 16, 128), BF16),
        pltpu.VMEM((1200, 128), F32),
        pltpu.VMEM((1200, 128), F32),
        pltpu.SemaphoreType.DMA((9,)),
        pltpu.SemaphoreType.DMA((2, 8)),
        pltpu.SemaphoreType.DMA((2, 8)),
        pltpu.SemaphoreType.DMA((2,)),
    ]
    result = pl.pallas_call(
        functools.partial(kernel, sizes),
        out_shape=jax.ShapeDtypeStruct((4, 24, 8, 128), BF16),
        in_specs=[hbm] * 9,
        out_specs=vmem,
        scratch_shapes=scratch,
        compiler_params=pltpu.CompilerParams(
            collective_id=0, has_side_effects=True, vmem_limit_bytes=60 << 20),
        cost_estimate=pl.CostEstimate(flops=3_000_000_000, bytes_accessed=6_000_000, transcendentals=300_000),
    )(tiles(video), tiles(cache_in), tiles(cache_mid), line(gain_in), line(gain_mid),
      taps(conv_in), line(bias_in), taps(conv_mid), line(bias_mid))
    return result.transpose(0, 2, 1, 3).reshape(video.shape)


def solution(mesh):
    tile = P("slab", "row", "col")
    cache = P(None, "row", "col")
    sizes = (mesh.shape["row"], mesh.shape["col"])
    return jax.shard_map(
        functools.partial(body, sizes), mesh=mesh,
        in_specs=(tile, cache, cache, P(), P(), P(), P(), P(), P()),
        out_specs=tile, check_vma=False)
```

time: 159 us -> 30.5 us (0.19)
  the two profiles are of different devices: /device:TPU:70 before, /device:TPU:1 now
where the time goes in v2:
time: 30.5 us; the launch traced here: 30.3 us
  Pallas kernels  28.7 us (94%)
  local copies, waits for them, and re-layouts  1.62 us (5%)
    pallas_call x1, Pallas kernels, body(): pl.pallas_call(functools.partial(kernel, sizes), out_shape=jax.ShapeDtype...  28.7 us
    unnamed x1, local copies, waits for them, and re-layouts  1.62 us

profile of v2, /device:TPU:1, one launch (start us, length us, event | category | flops | bytes accessed | tf_op | source)
XLA Modules:
  0.0 30.3 jit_solution(12920799715468295935)
XLA Ops:
  0.0 28.7 %shard_map.91 = bf16[4,24,8,128]{3,2,1,0:T(8,128)(2,1)} custom-call(bf16[4,24,8,128]{3,2,1,0:T(8,128)(2,1)} %bitcast.25, bf16[2,24,8,128]{3,2,1,0:T(8,128)(2,1)} %bitcast.26, bf16[2,24,8,128]{3,2,1,0:T(8,128)(2,1)} %bitcast.27, f32[1,192]{1,0:T(1,128)} %bitcast.28, f32[1,192]{1,0:T(1,128)} %bitcast.29, bf16[3,864,3,128]{3,2,1,0:T(4,128)(2,1)} %bitcast.23, ...), custom_call_target="tpu_custom_call" | custom-call | flops 3000000000 | bytes 6000000 | tf_op jit(solution)/shard_map/pallas_call | solution.py:514
  28.7 1.6 %copy.11 = bf16[4,8,3072]{2,1,0:T(8,128)(2,1)} copy(bf16[4,8,3072]{2,1,0:T(8,128)(2,1)} %bitcast.22) | data formatting | bytes 393216

commit v3 on v2

--- a/solution.py
+++ b/solution.py
@@ -43,32 +43,26 @@
     order[...] = jnp.where(c == source, 1.0, 0.0).astype(BF16)
 
 
-def lay_out_weights(raw, wide, out):
-    per = wide.shape[0] // 24
+def lay_out_weights(raw, wide, out, a, q):
     lanes = low_lanes((8, 128))
     flat = wide.reshape(wide.shape[0] * 8, 128)
-    out[:, 13 * 128 : 13 * 128 + 64, :] = jnp.zeros((3, 64, 256), BF16)
-
-    def step(n, _):
-        a, part = n // (36 // per), n % (36 // per)
-        for u in range(per):
-            g = part * per + u
-            wide[pl.ds(u * 24, 24), 0:3, :] = raw[a, pl.ds(g * 24, 24)].astype(F32)
-            q, group = g // 12, g % 12
-            for p in range(3):
-                first = flat[pl.ds(u * 192 + p, 8, stride=24)]
-                both = flat[pl.ds(u * 192 + 8 + p, 8, stride=24)]
-                second = swap(flat[pl.ds(u * 192 + 16 + p, 8, stride=24)])
-                odd = jnp.where(lanes, swap(both), second)
-                row_a = (p * 3 + q) * 128 + 16 * group
-                row_b = (9 + q) * 128 + 64 * p if p < 2 else 12 * 128 + 64 * q + jnp.where(q == 2, 64, 0)
-                row = jnp.where(group < 8, row_a, row_b + 16 * (group - 8))
+    for group in range(12):
+        wide[pl.ds(group * 24, 24), 0:3, :] = raw[a, pl.ds((q * 12 + group) * 24, 24)].astype(F32)
+        for p in range(3):
+            first = flat[pl.ds(group * 192 + p, 8, stride=24)]
+            both = flat[pl.ds(group * 192 + 8 + p, 8, stride=24)]
+            second = swap(flat[pl.ds(group * 192 + 16 + p, 8, stride=24)])
+            odd = jnp.where(lanes, swap(both), second)
+            if group < 8:
+                row = (p * 3 + q) * 128 + 16 * group
+            elif p < 2:
+                row = (9 + q) * 128 + 64 * p + 16 * (group - 8)
+            else:
+                row = 12 * 128 + 64 * (q + q // 2) + 16 * (group - 8)
+            if not isinstance(row, int):
                 row = pl.multiple_of(row, 16)
-                out[a, pl.ds(row, 16), 0:128] = jnp.concatenate([first, odd], 0).astype(BF16)
-                out[a, pl.ds(row, 16), 128:256] = jnp.concatenate([both, second], 0).astype(BF16)
-        return 0
-
-    lax.fori_loop(0, 3 * 36 // per, step, 0)
+            out[a, pl.ds(row, 16), 0:128] = jnp.concatenate([first, odd], 0).astype(BF16)
+            out[a, pl.ds(row, 16), 128:256] = jnp.concatenate([both, second], 0).astype(BF16)
 
 
 def split_columns(t0, t1, t2, lanes):
@@ -76,43 +70,37 @@
     return [(t0, t1), (jnp.where(lanes, t1s, t2s), t2s)]
 
 
-def gather_taps(sa, sb, ta, tb, start_of, step, apart, pairs, rows, cols):
+def gather_taps(sa, sb, ta, zp, zq, start_of, step, apart, pairs, rows, cols):
     size = start_of(1, 0, 0) - start_of(0, 0, 0)
+    lanes = low_lanes((16, 128))
 
     def tile(s, at):
         first = s[pl.ds(at, 8, stride=step), :]
         second = s[pl.ds(at + apart * size, 8, stride=step), :]
         return jnp.concatenate([first, second], 0).astype(BF16)
 
-    def body(n, _):
-        g, i = n // rows, n % rows
-        for j in range(cols):
-            at = start_of(g, i, j)
-            ta[g, i, j] = tile(sa, at)
-            tb[g, i, j] = tile(sb, at)
+    def body(g, _):
+        last = None
+        for i in range(rows):
+            for j in range(cols):
+                ta[g, i, j] = tile(sa, start_of(g, i, j))
+            now = [tile(sb, start_of(g, i, j)) for j in range(cols)]
+            if i > 0 and i < rows - 1:
+                for j in range(cols):
+                    zp[g, i - 1, j] = jnp.where(lanes, last[j], now[j])
+            if i > 1:
+                for j in range(cols - 1):
+                    zq[g, i - 2, j] = jnp.where(lanes, now[j], now[j + 1])
+            last = now
         return 0
 
-    lax.fori_loop(0, pairs * rows, body, 0)
-
-
-def merge_taps(tb, zp, zq, pairs, rows, cols):
-    lanes = low_lanes((16, 128))
-
-    def body(n, _):
-        g, i = n // rows, n % rows
-        for j in range(cols):
-            zp[g, i, j] = jnp.where(lanes, tb[g, i, j], tb[g, i + 1, j])
-        for j in range(cols - 1):
-            zq[g, i, j] = jnp.where(lanes, tb[g, i + 2, j], tb[g, i + 2, j + 1])
-        return 0
-
-    lax.fori_loop(0, pairs * rows, body, 0)
-
-
-def convolve(ta, zp, zq, weights, pairs, rows, cols):
+    lax.fori_loop(0, pairs, body, 0)
+
+
+def convolve(ta, zp, zq, weights, k, pairs, rows, cols):
     columns = []
     for a in range(3):
-        g = slice(a, a + pairs)
+        g = pl.ds(k + a, pairs)
         columns += [ta[g, p : p + rows, q : q + cols] for p in range(3) for q in range(3)]
         columns += [zp[g, :, q : q + cols] for q in range(3)]
         columns += [zq[g, :, q : q + cols] for q in range(2)]
@@ -124,7 +112,7 @@
 def kernel(sizes, video_hbm, cin_hbm, cmid_hbm, gin_hbm, gmid_hbm, win_hbm, bin_hbm, wmid_hbm, bmid_hbm, out,
            gain_in, gain_mid, bias_in, bias_mid, video, cin, cmid, raw_in, raw_mid, w_in, w_mid, wide, mixed, order,
            oa, ob, corner, sa, sb, ma, mb, tile, side, angle, got_tile, got_row, got_side, got_angle,
-           ta, tb, zp, zq, ua, ub, vp, vq, total_a, total_b,
+           ta, zp, zq, ua, vp, vq, total_a, total_b,
            load_sem, send_sem, recv_sem, tile_sem):
     n_row, n_col = sizes
     slab, row, col = lax.axis_index("slab"), lax.axis_index("row"), lax.axis_index("col")
@@ -171,9 +159,8 @@
     gain_a, gain_b = halves(gain_in)
 
     def activate_frame(n, _):
-        f = n // 2
-        for k in range(4):
-            j = (n % 2) * 4 + k
+        f = n
+        for j in range(8):
             put_mixed(f, j, [act(a, b, gain_a, gain_b, lanes8) for a, b in columns_of(video, f, j)])
         return 0
 
@@ -256,7 +243,7 @@
 
         lax.fori_loop(0, 4, frame, 0)
 
-    lax.fori_loop(0, 8, activate_frame, 0)
+    lax.fori_loop(0, 4, activate_frame, 0)
     reorder()
     pack(0)
     pl.semaphore_wait(barrier, greetings)
@@ -268,7 +255,7 @@
         to_partner.start()
 
     place_tile(4)
-    lax.fori_loop(0, 8, mix_caches, 0)
+    lax.fori_loop(0, 8, mix_caches, 0, unroll=4)
     reorder()
 
     @pl.when(slab == 1)
@@ -281,10 +268,16 @@
     def _():
         place_tile(0)
 
+    for w in (w_in, w_mid):
+        w[:, 13 * 128 : 13 * 128 + 64, :] = jnp.zeros((3, 64, 256), BF16)
     loads[7].wait()
-    lay_out_weights(raw_in, wide, w_in)
+
+    def lay_out_part(n, _):
+        lay_out_weights(raw_in, wide, w_in, n // 3, n % 3)
+        return 0
+
+    lax.fori_loop(0, 9, lay_out_part, 0)
     loads[8].wait()
-    lay_out_weights(raw_mid, wide, w_mid)
 
     def clear(x, has):
         return jnp.where(has, x, 0.0)
@@ -365,40 +358,36 @@
     def start_in(g, i, j):
         return (g * 13 + i + PAD) * LINE + j
 
-    gather_taps(sa, sb, ta, tb, start_in, 5, 3, 5, 7, 7)
-    merge_taps(tb, zp, zq, 5, 5, 7)
-    result = convolve(ta, zp, zq, w_in, 3, 5, 5)
-    total_a[...] = result[:, 0:128]
-    total_b[...] = result[:, 128:256]
-
+    gather_taps(sa, sb, ta, zp, zq, start_in, 5, 3, 5, 7, 7)
     bias_a, bias_b = halves(bias_in)
     gain_a, gain_b = halves(gain_mid)
     subs = lax.broadcasted_iota(jnp.int32, (16, 128), 0) & 7
-    ones = jnp.ones((16, 128), F32)
-
-    def activate_middle(n, _):
-        i = n % 5
-        gone = ((i == 0) & jnp.logical_not(up) & (subs < 4)) | ((i == 4) & jnp.logical_not(down) & (subs >= 4))
-        keep_rows = jnp.where(gone, 0.0, ones)
-        for j in range(5):
-            start = pl.multiple_of(n * 80 + j * 16, 16)
-            a = total_a[pl.ds(start, 16), :] + bias_a
-            b = total_b[pl.ds(start, 16), :] + bias_b
-            ya, yb = act(a, b, gain_a, gain_b, lanes16)
-            keep = keep_rows
-            if j == 0:
-                keep = jnp.where(jnp.logical_not(left) & ((subs & 3) == 0), 0.0, keep)
-            if j == 2:
-                keep = jnp.where(jnp.logical_not(right) & ((subs & 3) == 3), 0.0, keep)
-            mixed[pl.ds(start, 16), 0:128] = (ya * keep).astype(BF16)
-            mixed[pl.ds(start, 16), 128:256] = (yb * keep).astype(BF16)
-        return 0
-
-    lax.fori_loop(0, 15, activate_middle, 0)
-
-    def place_middle(k, _):
-        start = pl.multiple_of(k * 400, 16)
-        ordered = jnp.dot(mixed[pl.ds(start, 400), :], order[...], preferred_element_type=F32)
+
+    def middle_pair(k, _):
+        result = convolve(ta, zp, zq, w_in, k, 1, 5, 5)
+        for q in range(3):
+            lay_out_weights(raw_mid, wide, w_mid, k, q)
+        total_a[0:400] = result[:, 0:128]
+        total_b[0:400] = result[:, 128:256]
+        for i in range(5):
+            for j in range(5):
+                at = (i * 5 + j) * 16
+                ya, yb = act(total_a[at : at + 16, :] + bias_a, total_b[at : at + 16, :] + bias_b, gain_a, gain_b, lanes16)
+                gone = []
+                if i == 0:
+                    gone.append(jnp.logical_not(up) & (subs < 4))
+                if i == 4:
+                    gone.append(jnp.logical_not(down) & (subs >= 4))
+                if j == 0:
+                    gone.append(jnp.logical_not(left) & ((subs & 3) == 0))
+                if j == 2:
+                    gone.append(jnp.logical_not(right) & ((subs & 3) == 3))
+                if gone:
+                    gone = functools.reduce(jnp.logical_or, gone)
+                    ya, yb = jnp.where(gone, 0.0, ya), jnp.where(gone, 0.0, yb)
+                mixed[at : at + 16, 0:128] = ya.astype(BF16)
+                mixed[at : at + 16, 128:256] = yb.astype(BF16)
+        ordered = jnp.dot(mixed[0:400], order[...], preferred_element_type=F32)
         for n in range(25):
             for h in range(2):
                 at = (k + 3 * h) * MIDDLE + (n // 5) * LINE + n % 5
@@ -407,7 +396,7 @@
                 mb[pl.ds(at, 8, stride=5), :] = y[:, 128:256]
         return 0
 
-    lax.fori_loop(0, 3, place_middle, 0)
+    lax.fori_loop(0, 3, middle_pair, 0)
 
     @pl.when(slab == 0)
     def _():
@@ -426,9 +415,8 @@
     def start_mid(g, i, j):
         return g * MIDDLE + (i % 5) * LINE + (i // 5) * HALF + j
 
-    gather_taps(ma, mb, ua, ub, start_mid, 2, 2, 4, 10, 4)
-    merge_taps(ub, vp, vq, 4, 8, 4)
-    result = convolve(ua, vp, vq, w_mid, 2, 8, 2)
+    gather_taps(ma, mb, ua, vp, vq, start_mid, 2, 2, 4, 10, 4)
+    result = convolve(ua, vp, vq, w_mid, 0, 2, 8, 2)
     total_a[0:512] = result[:, 0:128]
     total_b[0:512] = result[:, 128:256]
 
@@ -445,7 +433,7 @@
                 out[f, 3 * c + k] = (video[f, 3 * c + k].astype(F32) + branch).astype(BF16)
         return 0
 
-    lax.fori_loop(0, 8, restore, 0)
+    lax.fori_loop(0, 8, restore, 0, unroll=4)
 
     each(own, "wait_send")
     each(early_frames, "wait_send", slab == 0)
@@ -479,8 +467,8 @@
         pltpu.VMEM((3, 864, 3, 128), BF16),
         pltpu.VMEM((3, 14 * 128, 256), BF16),
         pltpu.VMEM((3, 14 * 128, 256), BF16),
-        pltpu.VMEM((4 * 24, 8, 128), F32),
-        pltpu.VMEM((1200, 256), BF16),
+        pltpu.VMEM((12 * 24, 8, 128), F32),
+        pltpu.VMEM((512, 256), BF16),
         pltpu.VMEM((256, 256), BF16),
         pltpu.VMEM((512, 128), F32),
         pltpu.VMEM((512, 128), F32),
@@ -497,15 +485,13 @@
         pltpu.VMEM((2, 2, 2, 3, 16, 128), BF16),
         pltpu.VMEM((2, 4, 2, 16, 128), BF16),
         pltpu.VMEM((5, 7, 7, 16, 128), BF16),
-        pltpu.VMEM((5, 7, 7, 16, 128), BF16),
         pltpu.VMEM((5, 5, 7, 16, 128), BF16),
         pltpu.VMEM((5, 5, 6, 16, 128), BF16),
         pltpu.VMEM((4, 10, 4, 16, 128), BF16),
-        pltpu.VMEM((4, 10, 4, 16, 128), BF16),
         pltpu.VMEM((4, 8, 4, 16, 128), BF16),
         pltpu.VMEM((4, 8, 3, 16, 128), BF16),
-        pltpu.VMEM((1200, 128), F32),
-        pltpu.VMEM((1200, 128), F32),
+        pltpu.VMEM((512, 128), F32),
+        pltpu.VMEM((512, 128), F32),
         pltpu.SemaphoreType.DMA((9,)),
         pltpu.SemaphoreType.DMA((2, 8)),
         pltpu.SemaphoreType.DMA((2, 8)),

time: 30.5 us -> 24.9 us (0.82)
  Pallas kernels: 28.7 us -> 23.1 us
    pallas_call x1, Pallas kernels: 28.7 us -> 23.1 us  [body(): pl.pallas_call(functools.partial(kernel, sizes), out_shape=jax.ShapeDtype...]
where the time goes in v3:
time: 24.9 us; the launch traced here: 24.8 us
  Pallas kernels  23.1 us (93%)
  local copies, waits for them, and re-layouts  1.62 us (7%)
    pallas_call x1, Pallas kernels, body(): pl.pallas_call(functools.partial(kernel, sizes), out_shape=jax.ShapeDtype...  23.1 us
    unnamed x1, local copies, waits for them, and re-layouts  1.62 us

profile of v3, /device:TPU:1, one launch (start us, length us, event | category | flops | bytes accessed | tf_op | source)
XLA Modules:
  0.0 24.8 jit_solution(5765682048715034624)
XLA Ops:
  0.0 23.1 %shard_map.91 = bf16[4,24,8,128]{3,2,1,0:T(8,128)(2,1)} custom-call(bf16[4,24,8,128]{3,2,1,0:T(8,128)(2,1)} %bitcast.25, bf16[2,24,8,128]{3,2,1,0:T(8,128)(2,1)} %bitcast.26, bf16[2,24,8,128]{3,2,1,0:T(8,128)(2,1)} %bitcast.27, f32[1,192]{1,0:T(1,128)} %bitcast.28, f32[1,192]{1,0:T(1,128)} %bitcast.29, bf16[3,864,3,128]{3,2,1,0:T(4,128)(2,1)} %bitcast.23, ...), custom_call_target="tpu_custom_call" | custom-call | flops 3000000000 | bytes 6000000 | tf_op jit(solution)/shard_map/pallas_call | solution.py:500
  23.1 1.6 %copy.11 = bf16[4,8,3072]{2,1,0:T(8,128)(2,1)} copy(bf16[4,8,3072]{2,1,0:T(8,128)(2,1)} %bitcast.22) | data formatting | bytes 393216

commit v4 on v3

--- a/solution.py
+++ b/solution.py
@@ -16,6 +16,7 @@
 IMAGE = 13 * LINE
 MIDDLE = 5 * LINE
 AROUND = [(-1, 0), (1, 0), (0, -1), (0, 1), (-1, -1), (-1, 1), (1, -1), (1, 1)]
+FAR_FIRST = [4, 5, 6, 7, 2, 3, 0, 1]
 
 
 def low_lanes(shape):
@@ -31,7 +32,8 @@
     mean = jnp.sum(square, axis=1, keepdims=True) * (1.0 / CHAN)
     scale = lax.rsqrt(mean + 1e-6)
     ua, ub = a * scale * gain_a, b * scale * gain_b
-    return ua / (1.0 + jnp.exp(-ua)), ub / (1.0 + jnp.exp(-ub))
+    ua, ub = 0.5 * ua, 0.5 * ub
+    return ua + ua * jnp.tanh(ua), ub + ub * jnp.tanh(ub)
 
 
 def order_channels(order):
@@ -153,8 +155,8 @@
 
     def put_mixed(f, j, pixels):
         start = pl.multiple_of(f * 128 + j * 16, 16)
-        mixed[pl.ds(start, 16), 0:128] = jnp.concatenate([pixels[0][0], pixels[1][0]], 0).astype(BF16)
-        mixed[pl.ds(start, 16), 128:256] = jnp.concatenate([pixels[0][1], pixels[1][1]], 0).astype(BF16)
+        mixed[0, pl.ds(start, 16), 0:128] = jnp.concatenate([pixels[0][0], pixels[1][0]], 0).astype(BF16)
+        mixed[0, pl.ds(start, 16), 128:256] = jnp.concatenate([pixels[0][1], pixels[1][1]], 0).astype(BF16)
 
     gain_a, gain_b = halves(gain_in)
 
@@ -171,7 +173,7 @@
         return 0
 
     def reorder():
-        ordered = jnp.dot(mixed[0:512], order[...], preferred_element_type=F32)
+        ordered = jnp.dot(mixed[0], order[...], preferred_element_type=F32)
         oa[...] = ordered[:, 0:128]
         ob[...] = ordered[:, 128:256]
 
@@ -214,7 +216,7 @@
 
     def each(copies, method, condition=None):
         exist = [there[n] for n in (1, 0, 3, 2, 7, 6, 5, 4)] if method == "wait_recv" else there
-        for copy, has in zip(copies, exist):
+        for copy, has in [(copies[n], exist[n]) for n in FAR_FIRST]:
             @pl.when(has if condition is None else has & condition)
             def _():
                 getattr(copy, method)()
@@ -247,13 +249,13 @@
     reorder()
     pack(0)
     pl.semaphore_wait(barrier, greetings)
-    each(own, "start")
-    each(early_frames, "start", slab == 0)
-
     @pl.when(slab == 0)
     def _():
         to_partner.start()
 
+    each(own, "start")
+    each(early_frames, "start", slab == 0)
+
     place_tile(4)
     lax.fori_loop(0, 8, mix_caches, 0, unroll=4)
     reorder()
@@ -272,12 +274,16 @@
         w[:, 13 * 128 : 13 * 128 + 64, :] = jnp.zeros((3, 64, 256), BF16)
     loads[7].wait()
 
-    def lay_out_part(n, _):
-        lay_out_weights(raw_in, wide, w_in, n // 3, n % 3)
-        return 0
-
-    lax.fori_loop(0, 9, lay_out_part, 0)
+    def lay_out_all(raw, out):
+        def part(n, _):
+            lay_out_weights(raw, wide, out, n // 3, n % 3)
+            return 0
+
+        lax.fori_loop(0, 9, part, 0)
+
+    lay_out_all(raw_in, w_in)
     loads[8].wait()
+    lay_out_all(raw_mid, w_mid)
 
     def clear(x, has):
         return jnp.where(has, x, 0.0)
@@ -365,14 +371,13 @@
 
     def middle_pair(k, _):
         result = convolve(ta, zp, zq, w_in, k, 1, 5, 5)
-        for q in range(3):
-            lay_out_weights(raw_mid, wide, w_mid, k, q)
-        total_a[0:400] = result[:, 0:128]
-        total_b[0:400] = result[:, 128:256]
+        total_a[k, 0:400] = result[:, 0:128]
+        total_b[k, 0:400] = result[:, 128:256]
         for i in range(5):
             for j in range(5):
                 at = (i * 5 + j) * 16
-                ya, yb = act(total_a[at : at + 16, :] + bias_a, total_b[at : at + 16, :] + bias_b, gain_a, gain_b, lanes16)
+                ya, yb = act(
+                    total_a[k, at : at + 16, :] + bias_a, total_b[k, at : at + 16, :] + bias_b, gain_a, gain_b, lanes16)
                 gone = []
                 if i == 0:
                     gone.append(jnp.logical_not(up) & (subs < 4))
@@ -385,9 +390,9 @@
                 if gone:
                     gone = functools.reduce(jnp.logical_or, gone)
                     ya, yb = jnp.where(gone, 0.0, ya), jnp.where(gone, 0.0, yb)
-                mixed[at : at + 16, 0:128] = ya.astype(BF16)
-                mixed[at : at + 16, 128:256] = yb.astype(BF16)
-        ordered = jnp.dot(mixed[0:400], order[...], preferred_element_type=F32)
+                mixed[k, at : at + 16, 0:128] = ya.astype(BF16)
+                mixed[k, at : at + 16, 128:256] = yb.astype(BF16)
+        ordered = jnp.dot(mixed[k, 0:400], order[...], preferred_element_type=F32)
         for n in range(25):
             for h in range(2):
                 at = (k + 3 * h) * MIDDLE + (n // 5) * LINE + n % 5
@@ -416,24 +421,25 @@
         return g * MIDDLE + (i % 5) * LINE + (i // 5) * HALF + j
 
     gather_taps(ma, mb, ua, vp, vq, start_mid, 2, 2, 4, 10, 4)
-    result = convolve(ua, vp, vq, w_mid, 0, 2, 8, 2)
-    total_a[0:512] = result[:, 0:128]
-    total_b[0:512] = result[:, 128:256]
-
     bias_a, bias_b = halves(bias_mid)
 
-    def restore(c, _):
-        for f in range(4):
-            at = (f % 2) * 256 + (f // 2) * 8 + c
-            ae = total_a[pl.ds(at, 8, stride=32), :] + bias_a
-            be = total_b[pl.ds(at, 8, stride=32), :] + bias_b
-            ao = swap(total_a[pl.ds(at + 16, 8, stride=32), :] + bias_a)
-            bo = swap(total_b[pl.ds(at + 16, 8, stride=32), :] + bias_b)
-            for k, branch in enumerate((ae, jnp.where(lanes8, be, ao), jnp.where(lanes8, ao, bo))):
-                out[f, 3 * c + k] = (video[f, 3 * c + k].astype(F32) + branch).astype(BF16)
-        return 0
-
-    lax.fori_loop(0, 8, restore, 0, unroll=4)
+    def result_pair(k):
+        result = convolve(ua, vp, vq, w_mid, k, 1, 8, 2)
+        total_a[k, 0:256] = result[:, 0:128]
+        total_b[k, 0:256] = result[:, 128:256]
+        for h in range(2):
+            f = k + 2 * h
+            for c in range(8):
+                at = h * 8 + c
+                ae = total_a[k, pl.ds(at, 8, stride=32), :] + bias_a
+                be = total_b[k, pl.ds(at, 8, stride=32), :] + bias_b
+                ao = swap(total_a[k, pl.ds(at + 16, 8, stride=32), :] + bias_a)
+                bo = swap(total_b[k, pl.ds(at + 16, 8, stride=32), :] + bias_b)
+                for n, branch in enumerate((ae, jnp.where(lanes8, be, ao), jnp.where(lanes8, ao, bo))):
+                    out[f, 3 * c + n] = (video[f, 3 * c + n].astype(F32) + branch).astype(BF16)
+
+    for k in range(2):
+        result_pair(k)
 
     each(own, "wait_send")
     each(early_frames, "wait_send", slab == 0)
@@ -468,7 +474,7 @@
         pltpu.VMEM((3, 14 * 128, 256), BF16),
         pltpu.VMEM((3, 14 * 128, 256), BF16),
         pltpu.VMEM((12 * 24, 8, 128), F32),
-        pltpu.VMEM((512, 256), BF16),
+        pltpu.VMEM((3, 512, 256), BF16),
         pltpu.VMEM((256, 256), BF16),
         pltpu.VMEM((512, 128), F32),
         pltpu.VMEM((512, 128), F32),
@@ -490,8 +496,8 @@
         pltpu.VMEM((4, 10, 4, 16, 128), BF16),
         pltpu.VMEM((4, 8, 4, 16, 128), BF16),
         pltpu.VMEM((4, 8, 3, 16, 128), BF16),
-        pltpu.VMEM((512, 128), F32),
-        pltpu.VMEM((512, 128), F32),
+        pltpu.VMEM((3, 400, 128), F32),
+        pltpu.VMEM((3, 400, 128), F32),
         pltpu.SemaphoreType.DMA((9,)),
         pltpu.SemaphoreType.DMA((2, 8)),
         pltpu.SemaphoreType.DMA((2, 8)),
@@ -504,10 +510,11 @@
         out_specs=vmem,
         scratch_shapes=scratch,
         compiler_params=pltpu.CompilerParams(
-            collective_id=0, has_side_effects=True, vmem_limit_bytes=60 << 20),
+            collective_id=0, has_side_effects=True, vmem_limit_bytes=52 << 20),
         cost_estimate=pl.CostEstimate(flops=3_000_000_000, bytes_accessed=6_000_000, transcendentals=300_000),
-    )(tiles(video), tiles(cache_in), tiles(cache_mid), line(gain_in), line(gain_mid),
-      taps(conv_in), line(bias_in), taps(conv_mid), line(bias_mid))
+    )(*(pltpu.with_memory_space_constraint(x, pltpu.HBM) for x in (
+        tiles(video), tiles(cache_in), tiles(cache_mid), line(gain_in), line(gain_mid),
+        taps(conv_in), line(bias_in), taps(conv_mid), line(bias_mid))))
     return result.transpose(0, 2, 1, 3).reshape(video.shape)
 
 

time: 24.9 us -> 21.5 us (0.86)
  Pallas kernels: 23.1 us -> 20.8 us
  local copies, waits for them, and re-layouts: 1.62 us -> 0.68 us
    pallas_call x1, Pallas kernels: 23.1 us -> 20.8 us  [body(): pl.pallas_call(functools.partial(kernel, sizes), out_shape=jax.ShapeDtype...]
    unnamed x1, local copies, waits for them, and re-layouts: 1.62 us -> 0.68 us
where the time goes in v4:
time: 21.5 us; the launch traced here: 21.4 us
  Pallas kernels  20.8 us (97%)
  local copies, waits for them, and re-layouts  0.68 us (3%)
    pallas_call x1, Pallas kernels, body(): pl.pallas_call(functools.partial(kernel, sizes), out_shape=jax.ShapeDtype...  20.8 us
    unnamed x1, local copies, waits for them, and re-layouts  0.68 us

profile of v4, /device:TPU:1, one launch (start us, length us, event | category | flops | bytes accessed | tf_op | source)
XLA Modules:
  0.0 21.4 jit_solution(14546096404863352337)
XLA Ops:
  0.0 20.8 %shard_map.91 = bf16[4,24,8,128]{3,2,1,0:T(8,128)(2,1)S(1)} custom-call(bf16[4,24,8,128]{3,2,1,0:T(8,128)(2,1)} %bitcast.25, bf16[2,24,8,128]{3,2,1,0:T(8,128)(2,1)} %bitcast.26, bf16[2,24,8,128]{3,2,1,0:T(8,128)(2,1)} %bitcast.27, f32[1,192]{1,0:T(1,128)} %bitcast.28, f32[1,192]{1,0:T(1,128)} %bitcast.29, bf16[3,864,3,128]{3,2,1,0:T(4,128)(2,1)} %bitcast.23, ...), custom_call_target="tpu_custom_call" | custom-call | flops 3000000000 | bytes 6000000 | tf_op jit(solution)/shard_map/pallas_call | solution.py:506
  20.8 0.7 %copy.11 = bf16[4,8,3072]{2,1,0:T(8,128)(2,1)} copy(bf16[4,8,3072]{2,1,0:T(8,128)(2,1)S(1)} %bitcast.22) | data formatting | bytes 393216

commit v5 on v4

--- a/solution.py
+++ b/solution.py
@@ -72,7 +72,7 @@
     return [(t0, t1), (jnp.where(lanes, t1s, t2s), t2s)]
 
 
-def gather_taps(sa, sb, ta, zp, zq, start_of, step, apart, pairs, rows, cols):
+def gather_taps(sa, sb, ta, zp, zq, start_of, step, apart, first_pair, pairs, rows, cols):
     size = start_of(1, 0, 0) - start_of(0, 0, 0)
     lanes = low_lanes((16, 128))
 
@@ -96,7 +96,7 @@
             last = now
         return 0
 
-    lax.fori_loop(0, pairs, body, 0)
+    lax.fori_loop(first_pair, pairs, body, 0)
 
 
 def convolve(ta, zp, zq, weights, k, pairs, rows, cols):
@@ -121,8 +121,6 @@
     loads = [pltpu.make_async_copy(src, dst, load_sem.at[n]) for n, (src, dst) in enumerate(
         [(video_hbm, video), (cin_hbm, cin), (cmid_hbm, cmid), (gin_hbm, gain_in), (gmid_hbm, gain_mid),
          (bin_hbm, bias_in), (bmid_hbm, bias_mid), (win_hbm, raw_in), (wmid_hbm, raw_mid)])]
-    for load in loads:
-        load.start()
 
     up, down, left, right = row > 0, row < n_row - 1, col > 0, col < n_col - 1
     there = [up, down, left, right, up & left, up & right, down & left, down & right]
@@ -145,6 +143,9 @@
 
     def halves(ref):
         return ref[0:1, 0:128], jnp.concatenate([ref[0:1, 128:192], zero], 1)
+
+    for load in loads:
+        load.start()
 
     order_channels(order)
     for load in loads[:7]:
@@ -253,8 +254,8 @@
     def _():
         to_partner.start()
 
+    each(early_frames, "start", slab == 0)
     each(own, "start")
-    each(early_frames, "start", slab == 0)
 
     place_tile(4)
     lax.fori_loop(0, 8, mix_caches, 0, unroll=4)
@@ -364,13 +365,13 @@
     def start_in(g, i, j):
         return (g * 13 + i + PAD) * LINE + j
 
-    gather_taps(sa, sb, ta, zp, zq, start_in, 5, 3, 5, 7, 7)
+    gather_taps(sa, sb, ta, zp, zq, start_in, 5, 1, 2 - 2 * slab, 7, 7, 7)
     bias_a, bias_b = halves(bias_in)
     gain_a, gain_b = halves(gain_mid)
     subs = lax.broadcasted_iota(jnp.int32, (16, 128), 0) & 7
 
     def middle_pair(k, _):
-        result = convolve(ta, zp, zq, w_in, k, 1, 5, 5)
+        result = convolve(ta, zp, zq, w_in, 2 * k, 1, 5, 5)
         total_a[k, 0:400] = result[:, 0:128]
         total_b[k, 0:400] = result[:, 128:256]
         for i in range(5):
@@ -395,13 +396,13 @@
         ordered = jnp.dot(mixed[k, 0:400], order[...], preferred_element_type=F32)
         for n in range(25):
             for h in range(2):
-                at = (k + 3 * h) * MIDDLE + (n // 5) * LINE + n % 5
+                at = (2 * k + h) * MIDDLE + (n // 5) * LINE + n % 5
                 y = ordered[n * 16 + 8 * h : n * 16 + 8 * h + 8]
                 ma[pl.ds(at, 8, stride=5), :] = y[:, 0:128]
                 mb[pl.ds(at, 8, stride=5), :] = y[:, 128:256]
         return 0
 
-    lax.fori_loop(0, 3, middle_pair, 0)
+    lax.fori_loop(1 - slab, 3, middle_pair, 0)
 
     @pl.when(slab == 0)
     def _():
@@ -420,7 +421,7 @@
     def start_mid(g, i, j):
         return g * MIDDLE + (i % 5) * LINE + (i // 5) * HALF + j
 
-    gather_taps(ma, mb, ua, vp, vq, start_mid, 2, 2, 4, 10, 4)
+    gather_taps(ma, mb, ua, vp, vq, start_mid, 2, 2, 0, 4, 10, 4)
     bias_a, bias_b = halves(bias_mid)
 
     def result_pair(k):
@@ -490,9 +491,9 @@
         pltpu.VMEM((2, 2, 4, 3, 16, 128), BF16),
         pltpu.VMEM((2, 2, 2, 3, 16, 128), BF16),
         pltpu.VMEM((2, 4, 2, 16, 128), BF16),
-        pltpu.VMEM((5, 7, 7, 16, 128), BF16),
-        pltpu.VMEM((5, 5, 7, 16, 128), BF16),
-        pltpu.VMEM((5, 5, 6, 16, 128), BF16),
+        pltpu.VMEM((7, 7, 7, 16, 128), BF16),
+        pltpu.VMEM((7, 5, 7, 16, 128), BF16),
+        pltpu.VMEM((7, 5, 6, 16, 128), BF16),
         pltpu.VMEM((4, 10, 4, 16, 128), BF16),
         pltpu.VMEM((4, 8, 4, 16, 128), BF16),
         pltpu.VMEM((4, 8, 3, 16, 128), BF16),

time: 21.5 us -> 20.9 us (0.972)
  Pallas kernels: 20.8 us -> 20.1 us
    pallas_call x1, Pallas kernels: 20.8 us -> 20.1 us  [body(): pl.pallas_call(functools.partial(kernel, sizes), out_shape=jax.ShapeDtype...]
where the time goes in v5:
time: 20.9 us; the launch traced here: 20.8 us
  Pallas kernels  20.1 us (96%)
  local copies, waits for them, and re-layouts  0.68 us (3%)
    pallas_call x1, Pallas kernels, body(): pl.pallas_call(functools.partial(kernel, sizes), out_shape=jax.ShapeDtype...  20.1 us
    unnamed x1, local copies, waits for them, and re-layouts  0.68 us

profile of v5, /device:TPU:1, one launch (start us, length us, event | category | flops | bytes accessed | tf_op | source)
XLA Modules:
  0.0 20.8 jit_solution(3793664019766016812)
XLA Ops:
  0.0 20.1 %shard_map.91 = bf16[4,24,8,128]{3,2,1,0:T(8,128)(2,1)S(1)} custom-call(bf16[4,24,8,128]{3,2,1,0:T(8,128)(2,1)} %bitcast.25, bf16[2,24,8,128]{3,2,1,0:T(8,128)(2,1)} %bitcast.26, bf16[2,24,8,128]{3,2,1,0:T(8,128)(2,1)} %bitcast.27, f32[1,192]{1,0:T(1,128)} %bitcast.28, f32[1,192]{1,0:T(1,128)} %bitcast.29, bf16[3,864,3,128]{3,2,1,0:T(4,128)(2,1)} %bitcast.23, ...), custom_call_target="tpu_custom_call" | custom-call | flops 3000000000 | bytes 6000000 | tf_op jit(solution)/shard_map/pallas_call | solution.py:507
  20.1 0.7 %copy.11 = bf16[4,8,3072]{2,1,0:T(8,128)(2,1)} copy(bf16[4,8,3072]{2,1,0:T(8,128)(2,1)S(1)} %bitcast.22) | data formatting | bytes 393216

commit v6 on v5

--- a/solution.py
+++ b/solution.py
@@ -129,11 +129,11 @@
         return (s, lax.rem(row + dr + n_row, n_row), lax.rem(col + dc + n_col, n_col))
 
     barrier = pltpu.get_barrier_semaphore()
-    for s in range(2):
-        for (dr, dc), has in zip(AROUND, there):
-            @pl.when(has)
-            def _():
-                pl.semaphore_signal(barrier, inc=1, device_id=device(s, dr, dc), device_id_type=pl.DeviceIdType.MESH)
+    for n in FAR_FIRST:
+        @pl.when(there[n])
+        def _():
+            for s in range(2):
+                pl.semaphore_signal(barrier, inc=1, device_id=device(s, *AROUND[n]), device_id_type=pl.DeviceIdType.MESH)
     pl.semaphore_signal(barrier, inc=1, device_id=(1 - slab, row, col), device_id_type=pl.DeviceIdType.MESH)
     n_up_down, n_sides = up.astype(jnp.int32) + down.astype(jnp.int32), left.astype(jnp.int32) + right.astype(jnp.int32)
     greetings = 2 * (n_up_down + n_sides + n_up_down * n_sides) + 1

time: 20.9 us -> 20.9 us (level)
  no operation moved by 1% of the time
where the time goes in v6:
time: 20.9 us; the launch traced here: 20.8 us
  Pallas kernels  20.1 us (96%)
  local copies, waits for them, and re-layouts  0.68 us (3%)
    pallas_call x1, Pallas kernels, body(): pl.pallas_call(functools.partial(kernel, sizes), out_shape=jax.ShapeDtype...  20.1 us
    unnamed x1, local copies, waits for them, and re-layouts  0.68 us

profile of v6, /device:TPU:1, one launch (start us, length us, event | category | flops | bytes accessed | tf_op | source)
XLA Modules:
  0.0 20.8 jit_solution(3574385286568927015)
XLA Ops:
  0.0 20.1 %shard_map.91 = bf16[4,24,8,128]{3,2,1,0:T(8,128)(2,1)S(1)} custom-call(bf16[4,24,8,128]{3,2,1,0:T(8,128)(2,1)} %bitcast.25, bf16[2,24,8,128]{3,2,1,0:T(8,128)(2,1)} %bitcast.26, bf16[2,24,8,128]{3,2,1,0:T(8,128)(2,1)} %bitcast.27, f32[1,192]{1,0:T(1,128)} %bitcast.28, f32[1,192]{1,0:T(1,128)} %bitcast.29, bf16[3,864,3,128]{3,2,1,0:T(4,128)(2,1)} %bitcast.23, ...), custom_call_target="tpu_custom_call" | custom-call | flops 3000000000 | bytes 6000000 | tf_op jit(solution)/shard_map/pallas_call | solution.py:507
  20.1 0.7 %copy.11 = bf16[4,8,3072]{2,1,0:T(8,128)(2,1)} copy(bf16[4,8,3072]{2,1,0:T(8,128)(2,1)S(1)} %bitcast.22) | data formatting | bytes 393216
